TPU v7x, 256 devices: a whole 4x4x8 slice. The times are simulated.
256 devices in a mesh: ctx: 64 (over z, x, core), head: 4 (over y).
Axes of the slice: x: 4, y: 4, z: 8, core: 2. Of those that a mesh axis runs over, the one named last changes fastest.
Arguments:
- queries: bfloat16 [12288, 16384], P('ctx', 'head'), may hold values from -16 to 16
- keys: bfloat16 [12288, 1024], P('ctx', 'head'), may hold values from -16 to 16
- values: bfloat16 [12288, 1024], P('ctx', 'head'), may hold values from -6 to 6
- doc_lengths: int32 [128], replicated, may hold values from 1 to 2880, 12288 in all
Outputs:
- attended: bfloat16 [12288, 16384], P(('ctx', 'head'))
Inputs may be any that keep to these rules, and one draw needn't show every extreme that they name: `doc_lengths`: the longest document has exactly 2880 tokens.
All inputs are finite; a program needn't handle non-finite values.
Results may differ from a plain program's by a relative error of at most 0.0029.
Values may be sent and summed in bfloat16 or wider, within the bound.
A program may use at most 64 MiB of HBM per device.

v0:
```python
import jax
import jax.numpy as jnp
from jax import lax
from jax.sharding import PartitionSpec as P

HEAD_SIZE = 128


def passed_along(value, axis, steps):
    count = lax.axis_size(axis)
    leading, last = (max(0, -steps), min(count, count - steps))
    return lax.ppermute(value, axis, [(source, source + steps) for source in range(leading, last)])


def attend_group(query_part, key_part, value_part, allowed):
    scores = jnp.einsum(
        "qhd,kd->hqk", query_part, key_part, preferred_element_type=jnp.float32
    ) * HEAD_SIZE ** (-0.5)
    scores = jnp.where(allowed[None], scores, -1e30)
    highest = jnp.max(scores, axis=-1, keepdims=True)
    probs = jnp.where(allowed[None], jnp.exp(scores - highest), 0.0)
    totals = jnp.sum(probs, axis=-1)
    rounded = probs.astype(jnp.bfloat16)
    mixed = jnp.einsum("hqk,kd->qhd", rounded, value_part, preferred_element_type=jnp.float32)
    return (mixed / jnp.transpose(totals)[:, :, None]).astype(jnp.bfloat16)


def document_ids(doc_ends, positions):
    return jnp.sum((doc_ends[None, :] <= positions[:, None]).astype(jnp.int32), axis=1)


def per_device(queries, keys, values, doc_lengths):
    tok_rows = queries.shape[0]
    width_of_keys = keys.shape[1]
    hop_count = lax.axis_size("ctx") // 4
    ctx_place = lax.axis_index("ctx")
    own_block = jnp.stack([keys, values])
    window = jnp.concatenate(
        [jnp.zeros((2, (hop_count - 1) * tok_rows, width_of_keys), own_block.dtype), own_block],
        axis=1,
    )

    def relay_step(hop_index, carry_pair):
        collected, moving = carry_pair
        moving = passed_along(moving, "ctx", 1)
        slot_start = (hop_count - 2 - hop_index) * tok_rows
        collected = lax.dynamic_update_slice_in_dim(collected, moving, slot_start, 1)
        return (collected, moving)

    window, moving = lax.fori_loop(0, hop_count - 1, relay_step, (window, own_block))
    doc_ends = jnp.cumsum(doc_lengths)
    query_pos = ctx_place * tok_rows + jnp.arange(tok_rows, dtype=jnp.int32)
    key_pos = (ctx_place - hop_count + 1) * tok_rows + jnp.arange(
        hop_count * tok_rows, dtype=jnp.int32
    )
    query_docs = document_ids(doc_ends, query_pos)
    key_docs = jnp.where(key_pos >= 0, document_ids(doc_ends, key_pos), -1)
    allowed = (key_docs[None, :] == query_docs[:, None]) & (key_pos[None, :] <= query_pos[:, None])
    groups = width_of_keys // HEAD_SIZE
    per_group = queries.shape[1] // HEAD_SIZE // groups
    heads_item = 4
    item_count = groups * per_group // heads_item
    query_items = jnp.moveaxis(queries.reshape(tok_rows, item_count, heads_item, HEAD_SIZE), 1, 0)
    key_heads = window[0].reshape(hop_count * tok_rows, groups, HEAD_SIZE)
    value_heads = window[1].reshape(hop_count * tok_rows, groups, HEAD_SIZE)

    def one_item(item_index):
        group_index = item_index // (per_group // heads_item)
        return attend_group(
            query_items[item_index], key_heads[:, group_index], value_heads[:, group_index], allowed
        )

    mixed = lax.map(one_item, jnp.arange(item_count, dtype=jnp.int32))
    mixed = jnp.moveaxis(mixed, 0, 1).reshape(tok_rows, item_count * heads_item * HEAD_SIZE)
    return lax.all_to_all(mixed, "head", split_axis=0, concat_axis=1, tiled=True)


def solution(mesh):
    placed = (P("ctx", "head"), P("ctx", "head"), P("ctx", "head"), P())
    return jax.shard_map(
        per_device, mesh=mesh, in_specs=placed, out_specs=P(("ctx", "head"), None), check_vma=False
    )
```

profile of v0, /device:TPU:128, one launch (start us, length us, event | category | flops | bytes accessed | tf_op | source)
XLA Modules:
  0.0 334.9 jit_solution(958149482969775816)
XLA Ops:
  4.7 155.5 %while.28 = (s32[]{:T(128)}, bf16[2,3072,256]{2,1,0:T(8,128)(2,1)S(1)}, bf16[2,192,256]{2,1,0:T(8,128)(2,1)S(1)}, s32[]{:T(128)}, s32[]{:T(128)}, /*index=5*/s32[]{:T(128)}, s32[]{:T(128)}, s32[]{:T(128)}) while((s32[]{:T(128)}, bf16[2,3072,256]{2,1,0:T(8,128)(2,1)S(1)}, bf16[2,192,256]{2,1,0:T(8,128)(2,1)S(1)}, s32[]{:T(128)}, s32[]{:T(128)}, ...), condition=%wide.region_1.0_spmd, body=%wide.region_0.0_spmd.sunk | while | flops 7 | bytes 1573051 | solution.py:50
  6.7 8.4 %collective-permute-done = bf16[2,192,256]{2,1,0:T(8,128)(2,1)S(1)} collective-permute-done((bf16[2,192,256]{2,1,0:T(8,128)(2,1)S(1)}, bf16[2,192,256]{2,1,0:T(8,128)(2,1)S(1)}, u32[]{:S(2)}, u32[]{:S(2)}) %collective-permute-start) | collective-permute-done | bytes 196640 | tf_op jit(solution)/shard_map/while/body/eval_jaxpr/ppermute | solution.py:12
  17.0 8.4 %collective-permute-done = bf16[2,192,256]{2,1,0:T(8,128)(2,1)S(1)} collective-permute-done((bf16[2,192,256]{2,1,0:T(8,128)(2,1)S(1)}, bf16[2,192,256]{2,1,0:T(8,128)(2,1)S(1)}, u32[]{:S(2)}, u32[]{:S(2)}) %collective-permute-start) | collective-permute-done | bytes 196640 | tf_op jit(solution)/shard_map/while/body/eval_jaxpr/ppermute | solution.py:12
  27.4 8.4 %collective-permute-done = bf16[2,192,256]{2,1,0:T(8,128)(2,1)S(1)} collective-permute-done((bf16[2,192,256]{2,1,0:T(8,128)(2,1)S(1)}, bf16[2,192,256]{2,1,0:T(8,128)(2,1)S(1)}, u32[]{:S(2)}, u32[]{:S(2)}) %collective-permute-start) | collective-permute-done | bytes 196640 | tf_op jit(solution)/shard_map/while/body/eval_jaxpr/ppermute | solution.py:12
  37.8 8.4 %collective-permute-done = bf16[2,192,256]{2,1,0:T(8,128)(2,1)S(1)} collective-permute-done((bf16[2,192,256]{2,1,0:T(8,128)(2,1)S(1)}, bf16[2,192,256]{2,1,0:T(8,128)(2,1)S(1)}, u32[]{:S(2)}, u32[]{:S(2)}) %collective-permute-start) | collective-permute-done | bytes 196640 | tf_op jit(solution)/shard_map/while/body/eval_jaxpr/ppermute | solution.py:12
  48.1 8.4 %collective-permute-done = bf16[2,192,256]{2,1,0:T(8,128)(2,1)S(1)} collective-permute-done((bf16[2,192,256]{2,1,0:T(8,128)(2,1)S(1)}, bf16[2,192,256]{2,1,0:T(8,128)(2,1)S(1)}, u32[]{:S(2)}, u32[]{:S(2)}) %collective-permute-start) | collective-permute-done | bytes 196640 | tf_op jit(solution)/shard_map/while/body/eval_jaxpr/ppermute | solution.py:12
  58.5 8.4 %collective-permute-done = bf16[2,192,256]{2,1,0:T(8,128)(2,1)S(1)} collective-permute-done((bf16[2,192,256]{2,1,0:T(8,128)(2,1)S(1)}, bf16[2,192,256]{2,1,0:T(8,128)(2,1)S(1)}, u32[]{:S(2)}, u32[]{:S(2)}) %collective-permute-start) | collective-permute-done | bytes 196640 | tf_op jit(solution)/shard_map/while/body/eval_jaxpr/ppermute | solution.py:12
  68.9 8.4 %collective-permute-done = bf16[2,192,256]{2,1,0:T(8,128)(2,1)S(1)} collective-permute-done((bf16[2,192,256]{2,1,0:T(8,128)(2,1)S(1)}, bf16[2,192,256]{2,1,0:T(8,128)(2,1)S(1)}, u32[]{:S(2)}, u32[]{:S(2)}) %collective-permute-start) | collective-permute-done | bytes 196640 | tf_op jit(solution)/shard_map/while/body/eval_jaxpr/ppermute | solution.py:12
  79.2 8.4 %collective-permute-done = bf16[2,192,256]{2,1,0:T(8,128)(2,1)S(1)} collective-permute-done((bf16[2,192,256]{2,1,0:T(8,128)(2,1)S(1)}, bf16[2,192,256]{2,1,0:T(8,128)(2,1)S(1)}, u32[]{:S(2)}, u32[]{:S(2)}) %collective-permute-start) | collective-permute-done | bytes 196640 | tf_op jit(solution)/shard_map/while/body/eval_jaxpr/ppermute | solution.py:12
  89.6 8.4 %collective-permute-done = bf16[2,192,256]{2,1,0:T(8,128)(2,1)S(1)} collective-permute-done((bf16[2,192,256]{2,1,0:T(8,128)(2,1)S(1)}, bf16[2,192,256]{2,1,0:T(8,128)(2,1)S(1)}, u32[]{:S(2)}, u32[]{:S(2)}) %collective-permute-start) | collective-permute-done | bytes 196640 | tf_op jit(solution)/shard_map/while/body/eval_jaxpr/ppermute | solution.py:12
  100.0 8.4 %collective-permute-done = bf16[2,192,256]{2,1,0:T(8,128)(2,1)S(1)} collective-permute-done((bf16[2,192,256]{2,1,0:T(8,128)(2,1)S(1)}, bf16[2,192,256]{2,1,0:T(8,128)(2,1)S(1)}, u32[]{:S(2)}, u32[]{:S(2)}) %collective-permute-start) | collective-permute-done | bytes 196640 | tf_op jit(solution)/shard_map/while/body/eval_jaxpr/ppermute | solution.py:12
  110.4 8.4 %collective-permute-done = bf16[2,192,256]{2,1,0:T(8,128)(2,1)S(1)} collective-permute-done((bf16[2,192,256]{2,1,0:T(8,128)(2,1)S(1)}, bf16[2,192,256]{2,1,0:T(8,128)(2,1)S(1)}, u32[]{:S(2)}, u32[]{:S(2)}) %collective-permute-start) | collective-permute-done | bytes 196640 | tf_op jit(solution)/shard_map/while/body/eval_jaxpr/ppermute | solution.py:12
  120.7 8.4 %collective-permute-done = bf16[2,192,256]{2,1,0:T(8,128)(2,1)S(1)} collective-permute-done((bf16[2,192,256]{2,1,0:T(8,128)(2,1)S(1)}, bf16[2,192,256]{2,1,0:T(8,128)(2,1)S(1)}, u32[]{:S(2)}, u32[]{:S(2)}) %collective-permute-start) | collective-permute-done | bytes 196640 | tf_op jit(solution)/shard_map/while/body/eval_jaxpr/ppermute | solution.py:12
  131.1 8.4 %collective-permute-done = bf16[2,192,256]{2,1,0:T(8,128)(2,1)S(1)} collective-permute-done((bf16[2,192,256]{2,1,0:T(8,128)(2,1)S(1)}, bf16[2,192,256]{2,1,0:T(8,128)(2,1)S(1)}, u32[]{:S(2)}, u32[]{:S(2)}) %collective-permute-start) | collective-permute-done | bytes 196640 | tf_op jit(solution)/shard_map/while/body/eval_jaxpr/ppermute | solution.py:12
  141.5 8.4 %collective-permute-done = bf16[2,192,256]{2,1,0:T(8,128)(2,1)S(1)} collective-permute-done((bf16[2,192,256]{2,1,0:T(8,128)(2,1)S(1)}, bf16[2,192,256]{2,1,0:T(8,128)(2,1)S(1)}, u32[]{:S(2)}, u32[]{:S(2)}) %collective-permute-start) | collective-permute-done | bytes 196640 | tf_op jit(solution)/shard_map/while/body/eval_jaxpr/ppermute | solution.py:12
  151.8 8.4 %collective-permute-done = bf16[2,192,256]{2,1,0:T(8,128)(2,1)S(1)} collective-permute-done((bf16[2,192,256]{2,1,0:T(8,128)(2,1)S(1)}, bf16[2,192,256]{2,1,0:T(8,128)(2,1)S(1)}, u32[]{:S(2)}, u32[]{:S(2)}) %collective-permute-start) | collective-permute-done | bytes 196640 | tf_op jit(solution)/shard_map/while/body/eval_jaxpr/ppermute | solution.py:12
  168.6 143.1 %while.29 = (s32[]{:T(128)}, bf16[8,192,4,128]{3,1,2,0:T(8,128)(2,1)}, s32[8]{0:T(128)S(1)}, bf16[3072,2,128]{0,2,1:T(8,128)(2,1)}, bf16[3072,2,128]{0,2,1:T(8,1...) while((s32[]{:T(128)}, ...), condition=%wide.region_8.9_spmd.clone, body=%wide.region_5.8_spmd.clone.sunk | while | flops 1224084480 | bytes 13599102 | solution.py:73
  174.0 7.8 %fusion.61 = (f32[4,192]{1,0:T(4,128)S(1)}, bf16[4,192,3072]{2,1,0:T(8,128)(2,1)}) fusion(pred[192,3072]{1,0:T(8,128)(4,1)S(1)} %compare_and_fusion.2, bf16[3072,2,128]{0,2,1:T(8,128)(2,1)} %get-tuple-element.393, s32[]{:T(128)S(6)} %select_n.75, bf16[1,192,4,128]{3,2,0,1:T(4,128)(2,1)S(1)} %constant_dynamic-slice_fusion.2), kind=kOutput, calls=%fused_computation.38.clone.1 | convolution fusion | flops 618138624 | bytes 6884356 | tf_op jit(solution)/shard_map/while/body/eval_jaxpr/sub | solution.py:21
  191.9 7.8 %fusion.61 = (f32[4,192]{1,0:T(4,128)S(1)}, bf16[4,192,3072]{2,1,0:T(8,128)(2,1)}) fusion(pred[192,3072]{1,0:T(8,128)(4,1)S(1)} %compare_and_fusion.2, bf16[3072,2,128]{0,2,1:T(8,128)(2,1)} %get-tuple-element.393, s32[]{:T(128)S(6)} %select_n.75, bf16[1,192,4,128]{3,2,0,1:T(4,128)(2,1)S(1)} %constant_dynamic-slice_fusion.2), kind=kOutput, calls=%fused_computation.38.clone.1 | convolution fusion | flops 618138624 | bytes 6884356 | tf_op jit(solution)/shard_map/while/body/eval_jaxpr/sub | solution.py:21
  209.8 7.8 %fusion.61 = (f32[4,192]{1,0:T(4,128)S(1)}, bf16[4,192,3072]{2,1,0:T(8,128)(2,1)}) fusion(pred[192,3072]{1,0:T(8,128)(4,1)S(1)} %compare_and_fusion.2, bf16[3072,2,128]{0,2,1:T(8,128)(2,1)} %get-tuple-element.393, s32[]{:T(128)S(6)} %select_n.75, bf16[1,192,4,128]{3,2,0,1:T(4,128)(2,1)S(1)} %constant_dynamic-slice_fusion.2), kind=kOutput, calls=%fused_computation.38.clone.1 | convolution fusion | flops 618138624 | bytes 6884356 | tf_op jit(solution)/shard_map/while/body/eval_jaxpr/sub | solution.py:21
  227.7 7.8 %fusion.61 = (f32[4,192]{1,0:T(4,128)S(1)}, bf16[4,192,3072]{2,1,0:T(8,128)(2,1)}) fusion(pred[192,3072]{1,0:T(8,128)(4,1)S(1)} %compare_and_fusion.2, bf16[3072,2,128]{0,2,1:T(8,128)(2,1)} %get-tuple-element.393, s32[]{:T(128)S(6)} %select_n.75, bf16[1,192,4,128]{3,2,0,1:T(4,128)(2,1)S(1)} %constant_dynamic-slice_fusion.2), kind=kOutput, calls=%fused_computation.38.clone.1 | convolution fusion | flops 618138624 | bytes 6884356 | tf_op jit(solution)/shard_map/while/body/eval_jaxpr/sub | solution.py:21
  263.4 7.8 %fusion.61 = (f32[4,192]{1,0:T(4,128)S(1)}, bf16[4,192,3072]{2,1,0:T(8,128)(2,1)}) fusion(pred[192,3072]{1,0:T(8,128)(4,1)S(1)} %compare_and_fusion.2, bf16[3072,2,128]{0,2,1:T(8,128)(2,1)} %get-tuple-element.393, s32[]{:T(128)S(6)} %select_n.75, bf16[1,192,4,128]{3,2,0,1:T(4,128)(2,1)S(1)} %constant_dynamic-slice_fusion.2), kind=kOutput, calls=%fused_computation.38.clone.1 | convolution fusion | flops 618138624 | bytes 6884356 | tf_op jit(solution)/shard_map/while/body/eval_jaxpr/sub | solution.py:21
  281.3 7.8 %fusion.61 = (f32[4,192]{1,0:T(4,128)S(1)}, bf16[4,192,3072]{2,1,0:T(8,128)(2,1)}) fusion(pred[192,3072]{1,0:T(8,128)(4,1)S(1)} %compare_and_fusion.2, bf16[3072,2,128]{0,2,1:T(8,128)(2,1)} %get-tuple-element.393, s32[]{:T(128)S(6)} %select_n.75, bf16[1,192,4,128]{3,2,0,1:T(4,128)(2,1)S(1)} %constant_dynamic-slice_fusion.2), kind=kOutput, calls=%fused_computation.38.clone.1 | convolution fusion | flops 618138624 | bytes 6884356 | tf_op jit(solution)/shard_map/while/body/eval_jaxpr/sub | solution.py:21
  315.5 18.2 %all_to_all.19 = bf16[4,48,4096]{2,1,0:T(8,128)(2,1)S(1)} all-to-all(bf16[4,48,4096]{2,1,0:T(8,128)(2,1)S(1)} %all_to_all.14), channel_id=1, replica_groups=mesh['ctx'=64,'head'=4] {'head'}, dimensions={0} | all-to-all | bytes 3145728 | tf_op jit(solution)/shard_map/all_to_all | solution.py:75
  (101 shorter events, 110.2 us)
Async XLA Ops:
  4.7 10.3 %collective-permute-start = (bf16[2,192,256]{2,1,0:T(8,128)(2,1)S(1)}, bf16[2,192,256]{2,1,0:T(8,128)(2,1)S(1)}, u32[]{:S(2)}, u32[]{:S(2)}) collective-permute-start(bf16[2,192,256]{2,1,0:T(8,128)(2,1)S(1)} %get-tuple-element.343), channel_id=1, source_target_pairs={{0,4},{4,8},{8,12},{12,16},{16,20},{20,24},{24,28},{28,32},{32,36}... | collective-permute-start | bytes 589832 | tf_op jit(solution)/shard_map/while/body/eval_jaxpr/ppermute | solution.py:12
  15.1 10.3 %collective-permute-start = (bf16[2,192,256]{2,1,0:T(8,128)(2,1)S(1)}, bf16[2,192,256]{2,1,0:T(8,128)(2,1)S(1)}, u32[]{:S(2)}, u32[]{:S(2)}) collective-permute-start(bf16[2,192,256]{2,1,0:T(8,128)(2,1)S(1)} %get-tuple-element.343), channel_id=1, source_target_pairs={{0,4},{4,8},{8,12},{12,16},{16,20},{20,24},{24,28},{28,32},{32,36}... | collective-permute-start | bytes 589832 | tf_op jit(solution)/shard_map/while/body/eval_jaxpr/ppermute | solution.py:12
  25.5 10.3 %collective-permute-start = (bf16[2,192,256]{2,1,0:T(8,128)(2,1)S(1)}, bf16[2,192,256]{2,1,0:T(8,128)(2,1)S(1)}, u32[]{:S(2)}, u32[]{:S(2)}) collective-permute-start(bf16[2,192,256]{2,1,0:T(8,128)(2,1)S(1)} %get-tuple-element.343), channel_id=1, source_target_pairs={{0,4},{4,8},{8,12},{12,16},{16,20},{20,24},{24,28},{28,32},{32,36}... | collective-permute-start | bytes 589832 | tf_op jit(solution)/shard_map/while/body/eval_jaxpr/ppermute | solution.py:12
  35.8 10.3 %collective-permute-start = (bf16[2,192,256]{2,1,0:T(8,128)(2,1)S(1)}, bf16[2,192,256]{2,1,0:T(8,128)(2,1)S(1)}, u32[]{:S(2)}, u32[]{:S(2)}) collective-permute-start(bf16[2,192,256]{2,1,0:T(8,128)(2,1)S(1)} %get-tuple-element.343), channel_id=1, source_target_pairs={{0,4},{4,8},{8,12},{12,16},{16,20},{20,24},{24,28},{28,32},{32,36}... | collective-permute-start | bytes 589832 | tf_op jit(solution)/shard_map/while/body/eval_jaxpr/ppermute | solution.py:12
  46.2 10.3 %collective-permute-start = (bf16[2,192,256]{2,1,0:T(8,128)(2,1)S(1)}, bf16[2,192,256]{2,1,0:T(8,128)(2,1)S(1)}, u32[]{:S(2)}, u32[]{:S(2)}) collective-permute-start(bf16[2,192,256]{2,1,0:T(8,128)(2,1)S(1)} %get-tuple-element.343), channel_id=1, source_target_pairs={{0,4},{4,8},{8,12},{12,16},{16,20},{20,24},{24,28},{28,32},{32,36}... | collective-permute-start | bytes 589832 | tf_op jit(solution)/shard_map/while/body/eval_jaxpr/ppermute | solution.py:12
  56.6 10.3 %collective-permute-start = (bf16[2,192,256]{2,1,0:T(8,128)(2,1)S(1)}, bf16[2,192,256]{2,1,0:T(8,128)(2,1)S(1)}, u32[]{:S(2)}, u32[]{:S(2)}) collective-permute-start(bf16[2,192,256]{2,1,0:T(8,128)(2,1)S(1)} %get-tuple-element.343), channel_id=1, source_target_pairs={{0,4},{4,8},{8,12},{12,16},{16,20},{20,24},{24,28},{28,32},{32,36}... | collective-permute-start | bytes 589832 | tf_op jit(solution)/shard_map/while/body/eval_jaxpr/ppermute | solution.py:12
  66.9 10.3 %collective-permute-start = (bf16[2,192,256]{2,1,0:T(8,128)(2,1)S(1)}, bf16[2,192,256]{2,1,0:T(8,128)(2,1)S(1)}, u32[]{:S(2)}, u32[]{:S(2)}) collective-permute-start(bf16[2,192,256]{2,1,0:T(8,128)(2,1)S(1)} %get-tuple-element.343), channel_id=1, source_target_pairs={{0,4},{4,8},{8,12},{12,16},{16,20},{20,24},{24,28},{28,32},{32,36}... | collective-permute-start | bytes 589832 | tf_op jit(solution)/shard_map/while/body/eval_jaxpr/ppermute | solution.py:12
  77.3 10.3 %collective-permute-start = (bf16[2,192,256]{2,1,0:T(8,128)(2,1)S(1)}, bf16[2,192,256]{2,1,0:T(8,128)(2,1)S(1)}, u32[]{:S(2)}, u32[]{:S(2)}) collective-permute-start(bf16[2,192,256]{2,1,0:T(8,128)(2,1)S(1)} %get-tuple-element.343), channel_id=1, source_target_pairs={{0,4},{4,8},{8,12},{12,16},{16,20},{20,24},{24,28},{28,32},{32,36}... | collective-permute-start | bytes 589832 | tf_op jit(solution)/shard_map/while/body/eval_jaxpr/ppermute | solution.py:12
  87.7 10.3 %collective-permute-start = (bf16[2,192,256]{2,1,0:T(8,128)(2,1)S(1)}, bf16[2,192,256]{2,1,0:T(8,128)(2,1)S(1)}, u32[]{:S(2)}, u32[]{:S(2)}) collective-permute-start(bf16[2,192,256]{2,1,0:T(8,128)(2,1)S(1)} %get-tuple-element.343), channel_id=1, source_target_pairs={{0,4},{4,8},{8,12},{12,16},{16,20},{20,24},{24,28},{28,32},{32,36}... | collective-permute-start | bytes 589832 | tf_op jit(solution)/shard_map/while/body/eval_jaxpr/ppermute | solution.py:12
  98.0 10.3 %collective-permute-start = (bf16[2,192,256]{2,1,0:T(8,128)(2,1)S(1)}, bf16[2,192,256]{2,1,0:T(8,128)(2,1)S(1)}, u32[]{:S(2)}, u32[]{:S(2)}) collective-permute-start(bf16[2,192,256]{2,1,0:T(8,128)(2,1)S(1)} %get-tuple-element.343), channel_id=1, source_target_pairs={{0,4},{4,8},{8,12},{12,16},{16,20},{20,24},{24,28},{28,32},{32,36}... | collective-permute-start | bytes 589832 | tf_op jit(solution)/shard_map/while/body/eval_jaxpr/ppermute | solution.py:12
  108.4 10.3 %collective-permute-start = (bf16[2,192,256]{2,1,0:T(8,128)(2,1)S(1)}, bf16[2,192,256]{2,1,0:T(8,128)(2,1)S(1)}, u32[]{:S(2)}, u32[]{:S(2)}) collective-permute-start(bf16[2,192,256]{2,1,0:T(8,128)(2,1)S(1)} %get-tuple-element.343), channel_id=1, source_target_pairs={{0,4},{4,8},{8,12},{12,16},{16,20},{20,24},{24,28},{28,32},{32,36}... | collective-permute-start | bytes 589832 | tf_op jit(solution)/shard_map/while/body/eval_jaxpr/ppermute | solution.py:12
  118.8 10.3 %collective-permute-start = (bf16[2,192,256]{2,1,0:T(8,128)(2,1)S(1)}, bf16[2,192,256]{2,1,0:T(8,128)(2,1)S(1)}, u32[]{:S(2)}, u32[]{:S(2)}) collective-permute-start(bf16[2,192,256]{2,1,0:T(8,128)(2,1)S(1)} %get-tuple-element.343), channel_id=1, source_target_pairs={{0,4},{4,8},{8,12},{12,16},{16,20},{20,24},{24,28},{28,32},{32,36}... | collective-permute-start | bytes 589832 | tf_op jit(solution)/shard_map/while/body/eval_jaxpr/ppermute | solution.py:12
  129.2 10.3 %collective-permute-start = (bf16[2,192,256]{2,1,0:T(8,128)(2,1)S(1)}, bf16[2,192,256]{2,1,0:T(8,128)(2,1)S(1)}, u32[]{:S(2)}, u32[]{:S(2)}) collective-permute-start(bf16[2,192,256]{2,1,0:T(8,128)(2,1)S(1)} %get-tuple-element.343), channel_id=1, source_target_pairs={{0,4},{4,8},{8,12},{12,16},{16,20},{20,24},{24,28},{28,32},{32,36}... | collective-permute-start | bytes 589832 | tf_op jit(solution)/shard_map/while/body/eval_jaxpr/ppermute | solution.py:12
  139.5 10.3 %collective-permute-start = (bf16[2,192,256]{2,1,0:T(8,128)(2,1)S(1)}, bf16[2,192,256]{2,1,0:T(8,128)(2,1)S(1)}, u32[]{:S(2)}, u32[]{:S(2)}) collective-permute-start(bf16[2,192,256]{2,1,0:T(8,128)(2,1)S(1)} %get-tuple-element.343), channel_id=1, source_target_pairs={{0,4},{4,8},{8,12},{12,16},{16,20},{20,24},{24,28},{28,32},{32,36}... | collective-permute-start | bytes 589832 | tf_op jit(solution)/shard_map/while/body/eval_jaxpr/ppermute | solution.py:12
  149.9 10.3 %collective-permute-start = (bf16[2,192,256]{2,1,0:T(8,128)(2,1)S(1)}, bf16[2,192,256]{2,1,0:T(8,128)(2,1)S(1)}, u32[]{:S(2)}, u32[]{:S(2)}) collective-permute-start(bf16[2,192,256]{2,1,0:T(8,128)(2,1)S(1)} %get-tuple-element.343), channel_id=1, source_target_pairs={{0,4},{4,8},{8,12},{12,16},{16,20},{20,24},{24,28},{28,32},{32,36}... | collective-permute-start | bytes 589832 | tf_op jit(solution)/shard_map/while/body/eval_jaxpr/ppermute | solution.py:12
  163.3 4.1 %copy-start = (bf16[192,4096]{1,0:T(8,128)(2,1)S(1)}, bf16[192,4096]{1,0:T(8,128)(2,1)}, u32[]{:S(2)}) copy-start(bf16[192,4096]{1,0:T(8,128)(2,1)} %param.8) | copy-start | bytes 4718596
  167.2 1.4 copy-start.1
where the time goes:
time: 336 us; the launch traced here: 335 us
  waiting for transfers between devices  126 us (38%)
  matrix products  99.5 us (30%)
  loops' own time  34.1 us (10%)
  starting transfers between devices  28.8 us (9%)
  local copies, waits for them, and re-layouts  20.6 us (6%)
  blocking collectives  18.2 us (5%)
  other arithmetic  8.1 us (2%)
    ppermute x15, waiting for transfers between devices, passed_along(): lax.ppermute(value, axis, [(source, source + steps) for source in range(l...  126 us
    sub x8, matrix products, attend_group(): probs = jnp.where(allowed[None], jnp.exp(scores - highest), 0.0)  62.3 us
    dot_general x8, matrix products, attend_group(): jnp.einsum('hqk,kd->qhd', rounded, value_part, preferred_element_type=jnp...  37.2 us
    another operation x1, loops' own time, per_device(): mixed = lax.map(one_item, jnp.arange(item_count, dtype=jnp.int32))  33.4 us
    ppermute x15, starting transfers between devices, passed_along(): lax.ppermute(value, axis, [(source, source + steps) for source in range(l...  28.8 us
    all_to_all x1, blocking collectives, per_device(): lax.all_to_all(mixed, 'head', split_axis=0, concat_axis=1, tiled=True)  18.2 us
  transfers between devices with their start and end apart: 15, of which 15 were waited for; matrix products, arithmetic and copies ran while one was open for 0% of the time, Pallas kernels for 0%

commit v1 on v0

v1 whole, which is shorter than its diff:
```python
import math

import jax
import jax.numpy as jnp
from jax import lax
from jax.experimental import pallas as pl
from jax.experimental.pallas import tpu as pltpu
from jax.sharding import PartitionSpec as P

HEAD = 128
TOK = 192
GROUPS = 2
PER_GROUP = 16
SLOTS = 16
KEYS = SLOTS * TOK
PART = 4
BLOCKS = GROUPS * PER_GROUP // PART
ROWS = PART * TOK
CHUNK = 1536
EDGE = 256
OWN_TOK = 48
MINUS = -1e30
SCALE = HEAD**-0.5 * math.log2(math.e)
MESH = pl.DeviceIdType.MESH


def rows_of(slot):
    return pl.ds(pl.multiple_of(slot * TOK, TOK), TOK)


def kernel(
    q_hbm, k_hbm, v_hbm, len_ref, out_ref,
    kv, kc, kt, vx, s_ref, qv, ob, start_ref, first_ref, bias_ref,
    in_sem, send_sem, recv_sem, osend_sem, orecv_sem, olocal_sem,
):
    ctx = lax.axis_index("ctx")
    y = lax.axis_index("head")
    z = ctx // 8
    x = lax.rem(ctx // 2, 4)
    c = lax.rem(ctx, 2)
    left, right, across = lax.rem(x + 3, 4), lax.rem(x + 1, 4), lax.rem(x + 2, 4)

    def place(z_at, x_at, c_at):
        return (lax.rem(z_at + 8, 8) * 8 + x_at * 2 + c_at, y)

    sibling = place(z, x, 1 - c)
    up, down = place(z + 1, x, c), place(z - 1, x, c)
    to_left, to_right = place(z, left, c), place(z, right, c)
    over_y = [(ctx, lax.rem(y + r, 4)) for r in (1, 2, 3)]

    loads = []
    for g in range(GROUPS):
        for half, src in ((0, k_hbm), (1, v_hbm)):
            loads.append(pltpu.make_async_copy(
                src.at[:, pl.ds(g * HEAD, HEAD)],
                kv.at[g, pl.ds(0, TOK), pl.ds(half * HEAD, HEAD)],
                in_sem.at[2 * g + half]))
    q_load = pltpu.make_async_copy(q_hbm, qv, in_sem.at[4])
    for load in loads:
        load.start()
    q_load.start()

    barrier = pltpu.get_barrier_semaphore()
    partners = [sibling, up, down, to_left, to_right] + over_y
    for partner in partners:
        pl.semaphore_signal(barrier, inc=1, device_id=partner, device_id_type=MESH)
    pl.semaphore_wait(barrier, len(partners))
    for load in loads:
        load.wait()

    def near(frm, to):
        return lax.rem(2 * (to - frm) + 16, 16)

    def far(frm, to):
        return 8 + 2 * (to - frm)

    def copy(g, index, src, dst, target):
        return pltpu.make_async_remote_copy(
            src_ref=kv.at[g, rows_of(src), :], dst_ref=kv.at[g, rows_of(dst), :],
            send_sem=send_sem.at[g, index], recv_sem=recv_sem.at[g, dst],
            device_id=target, device_id_type=MESH)

    def arrived(g, slot):
        copy(g, 0, slot, slot, sibling).wait_recv()

    step = 1 - 2 * c
    own_or_old_right = jnp.where(x < 3, 0, 16)
    own_or_old_left = jnp.where(x > 0, 16, 0)
    on_right = (c == 0) & (x < 3) | (c == 1) & (x == 2)
    on_left = (c == 0) & (x == 1) | (c == 1) & (x > 0)

    def z_up(g): return copy(g, 0, 0, 8, up)
    def z_on(g): return copy(g, 1, 8, 16, up)
    def near_right(g): return copy(g, 2, own_or_old_right, near(x, right), to_right)
    def near_left(g): return copy(g, 3, own_or_old_left, near(x, left), to_left)
    def far_right(g): return copy(g, 4, 8, far(x, right), to_right)
    def far_left(g): return copy(g, 5, 8, far(x, left), to_left)
    def near_on_right(g): return copy(g, 6, near(left, x), near(left, right), to_right)
    def near_on_left(g): return copy(g, 7, near(right, x), near(right, left), to_left)
    def far_on(g):
        return copy(g, 8, jnp.where(c == 0, far(left, x), far(right, x)),
                    jnp.where(c == 0, far(left, right), far(right, left)),
                    place(z, jnp.where(c == 0, right, left), c))
    def aside(g, index, slot): return copy(g, 9 + index, slot, slot + step, sibling)
    def aside_own(g): return aside(g, 0, 16 * c)

    asides = [8, near(left, x), far(left, x), near(right, x), far(right, x),
              near(across, x), far(across, x)]

    def stage0(g):
        z_up(g).start()

        @pl.when(x < 3)
        def _():
            near_right(g).start()

        @pl.when(x == 0)
        def _():
            near_left(g).start()

        @pl.when(c == 0)
        def _():
            aside_own(g).start()

    def stage1(g):
        arrived(g, 8)
        z_on(g).start()
        far_right(g).start()
        far_left(g).start()
        aside(g, 1, 8).start()

    def stage2(g):
        arrived(g, 16)

        @pl.when(x == 3)
        def _():
            near_right(g).start()

        @pl.when(x > 0)
        def _():
            near_left(g).start()

        @pl.when(c == 1)
        def _():
            aside_own(g).start()

    def stage3(g):
        arrived(g, asides[1])

        @pl.when(on_right)
        def _():
            near_on_right(g).start()
        aside(g, 2, asides[1]).start()
        arrived(g, asides[3])

        @pl.when(on_left)
        def _():
            near_on_left(g).start()
        aside(g, 4, asides[3]).start()
        arrived(g, asides[2])
        arrived(g, asides[4])
        far_on(g).start()
        aside(g, 3, asides[2]).start()
        aside(g, 5, asides[4]).start()

    def stage4(g):
        arrived(g, asides[5])
        aside(g, 6, asides[5]).start()
        arrived(g, asides[6])
        aside(g, 7, asides[6]).start()

    def stage5(g):
        for slot in range(1, 16, 2):
            arrived(g, slot)

    def sent(g):
        for one in (z_up, z_on, near_right, near_left, far_right, far_left, far_on, aside_own):
            one(g).wait_send()

        @pl.when(on_right)
        def _():
            near_on_right(g).wait_send()

        @pl.when(on_left)
        def _():
            near_on_left(g).wait_send()
        for index, slot in enumerate(asides):
            aside(g, 1 + index, slot).wait_send()

    def documents():
        base = ctx * TOK
        lens = jnp.broadcast_to(len_ref[...].astype(jnp.float32), (128, 128))
        row = lax.broadcasted_iota(jnp.int32, (128, 128), 0)
        col = lax.broadcasted_iota(jnp.int32, (128, 128), 1)
        ends = jnp.sum(jnp.where(row <= col, lens.T, 0.0), axis=0, keepdims=True)
        here = (base + lax.broadcasted_iota(jnp.int32, (TOK, 128), 0)).astype(jnp.float32)
        start = jnp.max(jnp.where(ends <= here, ends, 0.0), axis=1, keepdims=True)
        offset = start - base.astype(jnp.float32)
        start_ref[...] = jnp.broadcast_to(offset[:8], (8, 128))
        first = offset < 0.0
        first_ref[...] = jnp.broadcast_to(jnp.where(first, 1.0, 0.0), (TOK, 128))
        i = lax.broadcasted_iota(jnp.int32, (TOK, EDGE), 0)
        j = lax.broadcasted_iota(jnp.int32, (TOK, EDGE), 1)
        inside = (j <= i) & (j.astype(jnp.float32) >= offset)
        rest = jnp.where(first, 0.0, MINUS)
        bias_ref[0] = jnp.where(j < TOK, jnp.where(inside, 0.0, MINUS), rest)
        bias_ref[1] = jnp.broadcast_to(rest, (TOK, EDGE))

    def prepare(g):
        stand_in = kv[g, 0:16, 0:HEAD].astype(jnp.float32)[0:1]
        begin = start_ref[0:1, :]

        def mask_slot(slot, carry):
            at = lax.broadcasted_iota(jnp.int32, (TOK, HEAD), 0) - slot * TOK
            keep = at.astype(jnp.float32) >= begin
            keep = keep | (slot == 0)
            k = kv[g, rows_of(slot), 0:HEAD].astype(jnp.float32)
            v = kv[g, rows_of(slot), HEAD:].astype(jnp.float32)
            kc[rows_of(slot), :] = jnp.where(keep, k, stand_in).astype(jnp.bfloat16)
            vx[g, rows_of(slot), 0:HEAD] = jnp.where(keep, v, 0.0).astype(jnp.bfloat16)
            vx[g, rows_of(slot), HEAD:] = jnp.where(keep, 1.0, 0.0).astype(jnp.bfloat16)
            return carry

        lax.fori_loop(0, SLOTS, mask_slot, 0)

        def turn(tile, carry):
            at = pl.ds(pl.multiple_of(tile * 128, 128), 128)
            turned = kc[at, :].T
            kt[g, 0:HEAD, at] = turned
            kt[g, HEAD:, at] = turned
            return carry

        lax.fori_loop(0, KEYS // 128, turn, 0)

    def out_copies(b):
        at = pl.ds(pl.multiple_of(y * 4096 + b * (PART * HEAD), PART * HEAD), PART * HEAD)
        remote = []
        for r in range(3):
            to = over_y[r]
            remote.append(pltpu.make_async_remote_copy(
                src_ref=ob.at[b, pl.ds(pl.multiple_of(to[1] * OWN_TOK, 16), OWN_TOK), :],
                dst_ref=out_ref.at[:, at],
                send_sem=osend_sem.at[b, r], recv_sem=orecv_sem.at[b, r],
                device_id=to, device_id_type=MESH))
        local = pltpu.make_async_copy(
            ob.at[b, pl.ds(pl.multiple_of(y * OWN_TOK, 16), OWN_TOK), :], out_ref.at[:, at],
            olocal_sem.at[b])
        return remote, local

    def block(b, carry):
        for when, what in ((1, lambda: (stage2(1), stage3(1))), (2, lambda: stage4(1)),
                           (3, lambda: stage5(1)), (4, lambda: prepare(1))):
            @pl.when(b == when)
            def _():
                what()

        g = b // (PER_GROUP // PART)
        parts = []
        for h in range(PART):
            at = pl.ds(pl.multiple_of((b * PART + h) * HEAD, HEAD), HEAD)
            scaled = qv[:, at].astype(jnp.float32) * SCALE
            high = scaled.astype(jnp.bfloat16)
            low = (scaled - high.astype(jnp.float32)).astype(jnp.bfloat16)
            parts.append(jnp.concatenate([high, low], axis=1))
        q = jnp.concatenate(parts, axis=0)
        least = jnp.full((ROWS, 128), MINUS, jnp.float32)

        def score(t, tops):
            edge_top, top = tops
            at = pl.multiple_of(t * CHUNK, CHUNK)
            s = jnp.dot(q, kt[g, :, pl.ds(at, CHUNK)], preferred_element_type=jnp.float32)
            edge = s[:, :EDGE] + jnp.concatenate([bias_ref[t]] * PART, axis=0)
            s_ref[:, pl.ds(at, EDGE)] = edge
            s_ref[:, pl.ds(at + EDGE, CHUNK - EDGE)] = s[:, EDGE:]
            edge_top = jnp.maximum(edge_top, jnp.maximum(edge[:, :128], edge[:, 128:]))
            for u in range(EDGE, CHUNK, 128):
                top = jnp.maximum(top, s[:, u:u + 128])
            return edge_top, top

        edge_top, top = lax.fori_loop(0, KEYS // CHUNK, score, (least, least))
        first = jnp.concatenate([first_ref[...]] * PART, axis=0)[:, :1] > 0.5
        top = jnp.where(first, jnp.max(top, axis=1, keepdims=True), MINUS)
        m = jnp.maximum(jnp.max(edge_top, axis=1, keepdims=True), top)
        m_rest = jnp.where(first, m, -MINUS)

        def mix(t, total):
            at = pl.multiple_of(t * CHUNK, CHUNK)
            edge = jnp.exp2(s_ref[:, pl.ds(at, EDGE)] - m).astype(jnp.bfloat16)
            rest = jnp.exp2(s_ref[:, pl.ds(at + EDGE, CHUNK - EDGE)] - m_rest).astype(jnp.bfloat16)
            p = jnp.concatenate([edge, rest], axis=1)
            return total + jnp.dot(p, vx[g, pl.ds(at, CHUNK), :], preferred_element_type=jnp.float32)

        total = lax.fori_loop(0, KEYS // CHUNK, mix, jnp.zeros((ROWS, 2 * HEAD), jnp.float32))
        o = (total[:, :HEAD] / total[:, HEAD:]).astype(jnp.bfloat16)
        for h in range(PART):
            ob[b, :, h * HEAD:(h + 1) * HEAD] = o[h * TOK:(h + 1) * TOK]
        remote, local = out_copies(b)
        for one in remote:
            one.start()
        local.start()
        return carry

    stage0(0)
    documents()
    stage1(0)
    stage2(0)
    stage3(0)
    stage0(1)
    stage4(0)
    stage1(1)
    stage5(0)
    prepare(0)
    q_load.wait()
    lax.fori_loop(0, BLOCKS, block, 0)

    def finish(b, carry):
        remote, local = out_copies(b)
        for one in remote:
            one.wait()
        local.wait()
        return carry

    lax.fori_loop(0, BLOCKS, finish, 0)
    for g in range(GROUPS):
        sent(g)


def per_device(queries, keys, values, doc_lengths):
    hbm = pl.BlockSpec(memory_space=pl.ANY)
    bf16, f32 = jnp.bfloat16, jnp.float32
    return pl.pallas_call(
        kernel,
        out_shape=jax.ShapeDtypeStruct((OWN_TOK, 4 * queries.shape[1]), bf16),
        in_specs=[hbm, hbm, hbm, pl.BlockSpec(memory_space=pltpu.VMEM)],
        out_specs=hbm,
        scratch_shapes=[
            pltpu.VMEM((GROUPS, (SLOTS + 1) * TOK, 2 * HEAD), bf16),
            pltpu.VMEM((KEYS, HEAD), bf16),
            pltpu.VMEM((GROUPS, 2 * HEAD, KEYS), bf16),
            pltpu.VMEM((GROUPS, KEYS, 2 * HEAD), bf16),
            pltpu.VMEM((ROWS, KEYS), f32),
            pltpu.VMEM((TOK, 4096), bf16),
            pltpu.VMEM((BLOCKS, TOK, PART * HEAD), bf16),
            pltpu.VMEM((8, 128), f32),
            pltpu.VMEM((TOK, 128), f32),
            pltpu.VMEM((KEYS // CHUNK, TOK, EDGE), f32),
            pltpu.SemaphoreType.DMA((5,)),
            pltpu.SemaphoreType.DMA((GROUPS, 17)),
            pltpu.SemaphoreType.DMA((GROUPS, 17)),
            pltpu.SemaphoreType.DMA((BLOCKS, 3)),
            pltpu.SemaphoreType.DMA((BLOCKS, 3)),
            pltpu.SemaphoreType.DMA((BLOCKS,)),
        ],
        compiler_params=pltpu.CompilerParams(
            collective_id=0, has_side_effects=True, vmem_limit_bytes=60 << 20),
    )(queries, keys, values, doc_lengths.reshape(1, 128))


def solution(mesh):
    placed = (P("ctx", "head"), P("ctx", "head"), P("ctx", "head"), P())
    return jax.shard_map(
        per_device, mesh=mesh, in_specs=placed, out_specs=P(("ctx", "head"), None), check_vma=False
    )
```

time: 336 us -> 80.9 us (0.24)
  the two profiles are of different devices: /device:TPU:128 before, /device:TPU:1 now
where the time goes in v1:
time: 80.9 us; the launch traced here: 80.8 us
  Pallas kernels  78.2 us (97%)
  local copies, waits for them, and re-layouts  2.65 us (3%)
    pallas_call x1, Pallas kernels, per_device(): pl.pallas_call(kernel, out_shape=jax.ShapeDtypeStruct((OWN_TOK, 4 * queri...  78.2 us
    unnamed x1, local copies, waits for them, and re-layouts  2.65 us

profile of v1, /device:TPU:1, one launch (start us, length us, event | category | flops | bytes accessed | tf_op | source)
XLA Modules:
  0.0 80.8 jit_solution(17902551847848723667)
XLA Ops:
  0.0 78.2 %shard_map.46 = bf16[48,16384]{1,0:T(8,128)(2,1)} custom-call(bf16[192,4096]{1,0:T(8,128)(2,1)} %q_hbm.1, bf16[192,256]{1,0:T(8,128)(2,1)} %k_hbm.1, bf16[192,256]{1,0:T(8,128)(2,1)} %v_hbm.1, s32[1,128]{1,0:T(1,128)} %bitcast.1), custom_call_target="tpu_custom_call" | custom-call | tf_op jit(solution)/shard_map/pallas_call | solution.py:331
  78.2 2.7 %copy.6 = bf16[48,16384]{1,0:T(8,128)(2,1)} copy(bf16[48,16384]{1,0:T(8,128)(2,1)} %shard_map.46) | data formatting | bytes 3145728

commit v2 on v1

v2 whole, which is shorter than its diff:
```python
import math

import jax
import jax.numpy as jnp
from jax import lax
from jax.experimental import pallas as pl
from jax.experimental.pallas import tpu as pltpu
from jax.sharding import PartitionSpec as P

HEAD = 128
TOK = 192
GROUPS = 2
PER_GROUP = 16
SLOTS = 16
KEYS = SLOTS * TOK
PART = 4
PARTS = PER_GROUP // PART
BLOCKS = GROUPS * PARTS
ROWS = PART * TOK
CHUNK = 1536
EDGE = 256
OWN_TOK = 48
MINUS = -1e30
SCALE = HEAD**-0.5 * math.log2(math.e)
MESH = pl.DeviceIdType.MESH


PLANES = 2 * GROUPS


def rows_of(slot):
    return pl.ds(pl.multiple_of(slot * TOK, TOK), TOK)


def kernel(
    q_hbm, k_hbm, v_hbm, len_ref, out_ref,
    kv, kc, kt, vx, s_ref, edge_ref, top_ref, qv, qs, ob, start_ref, first_ref, bias_ref,
    in_sem, send_sem, recv_sem, osend_sem, orecv_sem, olocal_sem,
):
    ctx = lax.axis_index("ctx")
    y = lax.axis_index("head")
    z = ctx // 8
    x = lax.rem(ctx // 2, 4)
    c = lax.rem(ctx, 2)

    def place(z_at, x_at, c_at):
        return (lax.rem(z_at + 8, 8) * 8 + x_at * 2 + c_at, y)

    sibling = place(z, x, 1 - c)
    others = [lax.rem(x + r, 4) for r in (1, 3, 2)]
    over_x = [place(z, to, c) for to in others]
    over_y = [(ctx, lax.rem(y + r, 4)) for r in (1, 2, 3)]
    aslant = [place(jnp.where(to < x, z + 1, z - 1), to, c) for to in others]

    loads = []
    for p in range(PLANES):
        loads.append(pltpu.make_async_copy(
            (k_hbm, v_hbm)[p % 2].at[:, pl.ds(p // 2 * HEAD, HEAD)],
            kv.at[p, pl.ds(0, TOK), :], in_sem.at[p]))
    q_load = pltpu.make_async_copy(q_hbm, qv, in_sem.at[PLANES])
    for load in loads:
        load.start()
    q_load.start()

    barrier = pltpu.get_barrier_semaphore()
    partners = [sibling] + [place(z + r, x, c) for r in (1, 2, -1, -2)] + over_x + over_y + aslant
    for partner in partners:
        pl.semaphore_signal(barrier, inc=1, device_id=partner, device_id_type=MESH)
    pl.semaphore_wait(barrier, len(partners))
    for load in loads:
        load.wait()

    def copy(p, index, src, dst, target):
        return pltpu.make_async_remote_copy(
            src_ref=kv.at[p, rows_of(src), :], dst_ref=kv.at[p, rows_of(dst), :],
            send_sem=send_sem.at[p, index], recv_sem=recv_sem.at[p, dst],
            device_id=target, device_id_type=MESH)

    def arrived(p, slot):
        copy(p, 0, slot, slot, sibling).wait_recv()

    def z_one(p): return copy(p, 0, 0, 8, place(z + 1, x, c))
    def z_two(p): return copy(p, 1, 0, 16, place(z + 2, x, c))

    def even(p, r):
        to = others[r]
        return copy(p, 2 + r, jnp.where(to > x, 0, 16), lax.rem(2 * (to - x) + 16, 16), over_x[r])

    def back(p, r):
        return copy(p, 5 + r, 8, 8 + 2 * (others[r] - x), over_x[r])

    def slanted(p, r):
        return copy(p, 5 + r, 0, 8 + 2 * (others[r] - x), aslant[r])

    def aside(p, slot): return copy(p, 8 + slot // 2, slot, slot + 1 - 2 * c, sibling)
    def aside_own(p): return copy(p, 8, 16 * c, 1 + 14 * c, sibling)

    def send_up(p):
        z_one(p).start()
        z_two(p).start()

    def send_row(p):
        for r in range(3):
            @pl.when(others[r] > x)
            def _():
                even(p, r).start()

        @pl.when(c == 0)
        def _():
            aside_own(p).start()

    def send_slanted(p):
        for r in range(3):
            @pl.when(others[r] < x)
            def _():
                slanted(p, r).start()

    def send_back(p):
        arrived(p, 8)
        for r in range(3):
            if p == 0:
                @pl.when(others[r] > x)
                def _():
                    back(p, r).start()
            else:
                back(p, r).start()
        aside(p, 8).start()

    def send_old(p):
        arrived(p, 16)
        for r in range(3):
            @pl.when(others[r] < x)
            def _():
                even(p, r).start()

        @pl.when(c == 1)
        def _():
            aside_own(p).start()

    def share(p, slots):
        for slot in slots:
            arrived(p, slot)
            aside(p, slot).start()

    def await_odd(p, slots):
        for slot in slots:
            arrived(p, slot)

    def sent(p):
        z_one(p).wait_send()
        z_two(p).wait_send()
        for r in range(3):
            even(p, r).wait_send()
            back(p, r).wait_send()
        aside_own(p).wait_send()
        for slot in range(2, 16, 2):
            aside(p, slot).wait_send()

    def documents():
        base = ctx * TOK
        lens = jnp.broadcast_to(len_ref[...].astype(jnp.float32), (128, 128))
        row = lax.broadcasted_iota(jnp.int32, (128, 128), 0)
        col = lax.broadcasted_iota(jnp.int32, (128, 128), 1)
        ends = jnp.sum(jnp.where(row <= col, lens.T, 0.0), axis=0, keepdims=True)
        here = (base + lax.broadcasted_iota(jnp.int32, (TOK, 128), 0)).astype(jnp.float32)
        start = jnp.max(jnp.where(ends <= here, ends, 0.0), axis=1, keepdims=True)
        offset = start - base.astype(jnp.float32)
        start_ref[...] = jnp.broadcast_to(offset[:8], (8, 128))
        first = offset < 0.0
        first_ref[...] = jnp.broadcast_to(jnp.where(first, 1.0, 0.0), (TOK, 128))
        i = lax.broadcasted_iota(jnp.int32, (TOK, EDGE), 0)
        j = lax.broadcasted_iota(jnp.int32, (TOK, EDGE), 1)
        inside = (j <= i) & (j.astype(jnp.float32) >= offset)
        rest = jnp.where(first, 0.0, MINUS)
        bias_ref[0] = jnp.where(j < TOK, jnp.where(inside, 0.0, MINUS), rest)
        bias_ref[1] = jnp.broadcast_to(rest, (TOK, EDGE))

    def scale_queries():
        def one(h, carry):
            scaled = qv[:, pl.ds(pl.multiple_of(h * HEAD, HEAD), HEAD)].astype(jnp.float32) * SCALE
            high = scaled.astype(jnp.bfloat16)
            qs[rows_of(h), 0:HEAD] = high
            qs[rows_of(h), HEAD:] = (scaled - high.astype(jnp.float32)).astype(jnp.bfloat16)
            return carry

        lax.fori_loop(0, GROUPS * PER_GROUP, one, 0)

    def kept(slot):
        at = lax.broadcasted_iota(jnp.int32, (TOK, HEAD), 0) - slot * TOK
        return (at.astype(jnp.float32) >= start_ref[0:1, :]) | (slot == 0)

    def prepare_keys(g, half):
        p = 2 * g
        stand_in = kv[p, 0:16, :].astype(jnp.float32)[0:1]

        def mask_slot(slot, carry):
            k = kv[p, rows_of(slot), :].astype(jnp.float32)
            kc[rows_of(slot), :] = jnp.where(kept(slot), k, stand_in).astype(jnp.bfloat16)
            return carry

        lax.fori_loop(half * 8, half * 8 + 8, mask_slot, 0)

        def turn(tile, carry):
            at = pl.ds(pl.multiple_of(tile * 128, 128), 128)
            turned = kc[at, :].T
            kt[g, 0:HEAD, at] = turned
            kt[g, HEAD:, at] = turned
            return carry

        lax.fori_loop(half * 12, half * 12 + 12, turn, 0)

    def prepare_values(g):
        def mask_slot(slot, carry):
            keep = kept(slot)
            v = kv[2 * g + 1, rows_of(slot), :].astype(jnp.float32)
            vx[g, rows_of(slot), 0:HEAD] = jnp.where(keep, v, 0.0).astype(jnp.bfloat16)
            vx[g, rows_of(slot), HEAD:] = jnp.where(keep, 1.0, 0.0).astype(jnp.bfloat16)
            return carry

        lax.fori_loop(0, SLOTS, mask_slot, 0)

    def out_copies(b):
        at = pl.ds(pl.multiple_of(y * 4096 + b * (PART * HEAD), PART * HEAD), PART * HEAD)
        remote = []
        for r in range(3):
            to = over_y[r]
            remote.append(pltpu.make_async_remote_copy(
                src_ref=ob.at[b, pl.ds(pl.multiple_of(to[1] * OWN_TOK, 16), OWN_TOK), :],
                dst_ref=out_ref.at[:, at],
                send_sem=osend_sem.at[b, r], recv_sem=orecv_sem.at[b, r],
                device_id=to, device_id_type=MESH))
        local = pltpu.make_async_copy(
            ob.at[b, pl.ds(pl.multiple_of(y * OWN_TOK, 16), OWN_TOK), :], out_ref.at[:, at],
            olocal_sem.at[b])
        return remote, local

    def score(b, t):
        g = b // PARTS
        kept_at = lax.rem(b, PARTS)
        into = jnp.where(t == 0, kept_at, PARTS)
        at = pl.multiple_of(t * CHUNK, CHUNK)
        q = qs[pl.ds(pl.multiple_of(b * ROWS, ROWS), ROWS), :]
        s = jnp.dot(q, kt[g, :, pl.ds(at, CHUNK)], preferred_element_type=jnp.float32)
        edge = s[:, :EDGE] + jnp.concatenate([bias_ref[t]] * PART, axis=0)
        s_ref[into, :, 0:EDGE] = edge
        s_ref[into, :, EDGE:] = s[:, EDGE:]
        edge_ref[t, kept_at] = jnp.maximum(edge[:, :128], edge[:, 128:])
        top = s[:, EDGE:EDGE + 128]
        for u in range(EDGE + 128, CHUNK, 128):
            top = jnp.maximum(top, s[:, u:u + 128])
        top_ref[t, kept_at] = top

    def near_scores(b, carry):
        for when, what in NEAR_STEPS:
            @pl.when(b == when)
            def _():
                what()
        score(b, 0)
        return carry

    def block(b, carry):
        for when, what in STEPS:
            @pl.when(b == when)
            def _():
                what()
        g = b // PARTS
        kept_at = lax.rem(b, PARTS)

        def score_on(t, carry):
            score(b, t)
            return carry

        lax.fori_loop(jnp.where(b < PARTS, 1, 0), 2, score_on, 0)
        for when, what in VALUE_STEPS:
            @pl.when(b == when)
            def _():
                what()
        first = jnp.concatenate([first_ref[...]] * PART, axis=0)[:, :1] > 0.5
        top = jnp.max(jnp.maximum(top_ref[0, kept_at], top_ref[1, kept_at]), axis=1, keepdims=True)
        edge_top = jnp.max(jnp.maximum(edge_ref[0, kept_at], edge_ref[1, kept_at]), axis=1, keepdims=True)
        m = jnp.maximum(edge_top, jnp.where(first, top, MINUS))
        m_rest = jnp.where(first, m, -MINUS)

        def mix(t, total):
            at = pl.multiple_of(t * CHUNK, CHUNK)
            frm = jnp.where(t == 0, kept_at, PARTS)
            edge = jnp.exp2(s_ref[frm, :, 0:EDGE] - m).astype(jnp.bfloat16)
            rest = jnp.exp2(s_ref[frm, :, EDGE:] - m_rest).astype(jnp.bfloat16)
            p = jnp.concatenate([edge, rest], axis=1)
            return total + jnp.dot(p, vx[g, pl.ds(at, CHUNK), :], preferred_element_type=jnp.float32)

        total = lax.fori_loop(0, 2, mix, jnp.zeros((ROWS, 2 * HEAD), jnp.float32))
        o = (total[:, :HEAD] / total[:, HEAD:]).astype(jnp.bfloat16)
        for h in range(PART):
            ob[b, :, h * HEAD:(h + 1) * HEAD] = o[h * TOK:(h + 1) * TOK]
        remote, local = out_copies(b)
        for one in remote:
            one.start()
        local.start()
        return carry

    near, far = (2, 4, 6), (10, 12, 14)
    odd_near, odd_far = (1, 3, 5, 7), (9, 11, 13, 15)
    NEAR_STEPS = (
        (1, lambda: share(0, far)),
        (2, lambda: send_up(2)),
        (3, lambda: send_row(2)),
    )
    STEPS = (
        (0, lambda: (share(1, near + far), await_odd(0, odd_far), prepare_keys(0, 1))),
        (1, lambda: (send_old(2), send_up(3))),
        (2, lambda: (send_row(3), send_back(3))),
        (3, lambda: await_odd(2, odd_near + odd_far)),
        (4, lambda: (prepare_keys(1, 0), prepare_keys(1, 1), share(3, near + far))),
    )
    VALUE_STEPS = (
        (0, lambda: (send_back(2), await_odd(1, odd_near + odd_far), prepare_values(0))),
        (2, lambda: (share(2, near + far), send_old(3))),
        (4, lambda: (await_odd(3, odd_near + odd_far), prepare_values(1))),
    )

    send_row(0)
    send_slanted(0)
    send_up(0)
    send_up(1)
    documents()
    q_load.wait()
    scale_queries()
    share(0, near)
    send_back(0)
    send_old(0)
    send_row(1)
    send_back(1)
    send_old(1)
    await_odd(0, odd_near)
    prepare_keys(0, 0)
    lax.fori_loop(0, PARTS, near_scores, 0)
    lax.fori_loop(0, BLOCKS, block, 0)

    def finish(b, carry):
        remote, local = out_copies(b)
        for one in remote:
            one.wait()
        local.wait()
        return carry

    lax.fori_loop(0, BLOCKS, finish, 0)
    for p in range(PLANES):
        sent(p)


def per_device(queries, keys, values, doc_lengths):
    hbm = pl.BlockSpec(memory_space=pl.ANY)
    bf16, f32 = jnp.bfloat16, jnp.float32
    return pl.pallas_call(
        kernel,
        out_shape=jax.ShapeDtypeStruct((OWN_TOK, 4 * queries.shape[1]), bf16),
        in_specs=[hbm, hbm, hbm, pl.BlockSpec(memory_space=pltpu.VMEM)],
        out_specs=hbm,
        scratch_shapes=[
            pltpu.VMEM((PLANES, (SLOTS + 1) * TOK, HEAD), bf16),
            pltpu.VMEM((KEYS, HEAD), bf16),
            pltpu.VMEM((GROUPS, 2 * HEAD, KEYS), bf16),
            pltpu.VMEM((GROUPS, KEYS, 2 * HEAD), bf16),
            pltpu.VMEM((PARTS + 1, ROWS, CHUNK), f32),
            pltpu.VMEM((2, PARTS, ROWS, 128), f32),
            pltpu.VMEM((2, PARTS, ROWS, 128), f32),
            pltpu.VMEM((TOK, 4096), bf16),
            pltpu.VMEM((GROUPS * PER_GROUP * TOK, 2 * HEAD), bf16),
            pltpu.VMEM((BLOCKS, TOK, PART * HEAD), bf16),
            pltpu.VMEM((8, 128), f32),
            pltpu.VMEM((TOK, 128), f32),
            pltpu.VMEM((2, TOK, EDGE), f32),
            pltpu.SemaphoreType.DMA((PLANES + 1,)),
            pltpu.SemaphoreType.DMA((PLANES, 16)),
            pltpu.SemaphoreType.DMA((PLANES, SLOTS + 1)),
            pltpu.SemaphoreType.DMA((BLOCKS, 3)),
            pltpu.SemaphoreType.DMA((BLOCKS, 3)),
            pltpu.SemaphoreType.DMA((BLOCKS,)),
        ],
        compiler_params=pltpu.CompilerParams(
            collective_id=0, has_side_effects=True, vmem_limit_bytes=60 << 20),
    )(queries, keys, values, doc_lengths.reshape(1, 128))


def solution(mesh):
    placed = (P("ctx", "head"), P("ctx", "head"), P("ctx", "head"), P())
    return jax.shard_map(
        per_device, mesh=mesh, in_specs=placed, out_specs=P(("ctx", "head"), None), check_vma=False
    )
```

time: 80.9 us -> 69.7 us (0.86)
  Pallas kernels: 78.2 us -> 66.9 us
    pallas_call x1, Pallas kernels: 78.2 us -> 66.9 us  [per_device(): pl.pallas_call(kernel, out_shape=jax.ShapeDtypeStruct((OWN_TOK, 4 * queri...]
where the time goes in v2:
time: 69.7 us; the launch traced here: 69.6 us
  Pallas kernels  66.9 us (96%)
  local copies, waits for them, and re-layouts  2.65 us (4%)
    pallas_call x1, Pallas kernels, per_device(): pl.pallas_call(kernel, out_shape=jax.ShapeDtypeStruct((OWN_TOK, 4 * queri...  66.9 us
    unnamed x1, local copies, waits for them, and re-layouts  2.65 us

profile of v2, /device:TPU:1, one launch (start us, length us, event | category | flops | bytes accessed | tf_op | source)
XLA Modules:
  0.0 69.6 jit_solution(4479285340058671781)
XLA Ops:
  0.0 66.9 %shard_map.46 = bf16[48,16384]{1,0:T(8,128)(2,1)} custom-call(bf16[192,4096]{1,0:T(8,128)(2,1)} %q_hbm.1, bf16[192,256]{1,0:T(8,128)(2,1)} %k_hbm.1, bf16[192,256]{1,0:T(8,128)(2,1)} %v_hbm.1, s32[1,128]{1,0:T(1,128)} %bitcast.1), custom_call_target="tpu_custom_call" | custom-call | tf_op jit(solution)/shard_map/pallas_call | solution.py:355
  66.9 2.7 %copy.6 = bf16[48,16384]{1,0:T(8,128)(2,1)} copy(bf16[48,16384]{1,0:T(8,128)(2,1)} %shard_map.46) | data formatting | bytes 3145728

commit v3 on v2

v3 whole, which is shorter than its diff:
```python
import math

import jax
import jax.numpy as jnp
from jax import lax
from jax.experimental import pallas as pl
from jax.experimental.pallas import tpu as pltpu
from jax.sharding import PartitionSpec as P

HEAD = 128
TOK = 192
GROUPS = 2
PER_GROUP = 16
SLOTS = 16
KEYS = SLOTS * TOK
PART = 4
PARTS = PER_GROUP // PART
BLOCKS = GROUPS * PARTS
ROWS = PART * TOK
CHUNK = 1536
EDGE = 256
OWN_TOK = 48
MINUS = -1e30
SCALE = HEAD**-0.5 * math.log2(math.e)
MESH = pl.DeviceIdType.MESH


PLANES = 2 * GROUPS


def rows_of(slot):
    return pl.ds(pl.multiple_of(slot * TOK, TOK), TOK)


def kernel(
    q_hbm, k_hbm, v_hbm, len_ref, out_ref,
    kv, s_ref, top_ref, m_ref, near_ref, qv, qs, ob, row_bias_ref, key_bias_ref, bias_ref,
    in_sem, above_sem, send_sem, recv_sem, osend_sem, orecv_sem, olocal_sem,
):
    ctx = lax.axis_index("ctx")
    y = lax.axis_index("head")
    z = ctx // 8
    x = lax.rem(ctx // 2, 4)
    c = lax.rem(ctx, 2)

    def place(z_at, x_at, c_at):
        return (lax.rem(z_at + 8, 8) * 8 + x_at * 2 + c_at, y)

    sibling = place(z, x, 1 - c)
    others = [lax.rem(x + r, 4) for r in (1, 3, 2)]
    over_x = [place(z, to, c) for to in others]
    over_y = [(ctx, lax.rem(y + r, 4)) for r in (1, 2, 3)]
    loads = []
    for p in range(PLANES):
        loads.append(pltpu.make_async_copy(
            (k_hbm, v_hbm)[p % 2].at[:, pl.ds(p // 2 * HEAD, HEAD)],
            kv.at[p, pl.ds(0, TOK), :], in_sem.at[p]))
    q_load = pltpu.make_async_copy(q_hbm, qv, in_sem.at[PLANES])
    for load in loads:
        load.start()
    q_load.start()

    barrier = pltpu.get_barrier_semaphore()
    above, below = place(z + 1, x, c), place(z - 1, x, c)
    has_above, has_below = z < 7, z > 0
    partners = [sibling] + over_x + over_y
    for partner in partners:
        pl.semaphore_signal(barrier, inc=1, device_id=partner, device_id_type=MESH)

    @pl.when(has_above)
    def _():
        pl.semaphore_signal(barrier, inc=1, device_id=above, device_id_type=MESH)

    pl.semaphore_wait(barrier, len(partners) + jnp.where(has_below, 1, 0))

    @pl.when(has_below)
    def _():
        pl.semaphore_signal(above_sem, inc=1, device_id=below, device_id_type=MESH)

    for load in loads:
        load.wait()

    def copy(p, index, src, dst, target):
        return pltpu.make_async_remote_copy(
            src_ref=kv.at[p, rows_of(src), :], dst_ref=kv.at[p, rows_of(dst), :],
            send_sem=send_sem.at[p, index], recv_sem=recv_sem.at[p, dst],
            device_id=target, device_id_type=MESH)

    def arrived(p, slot):
        copy(p, 0, slot, slot, sibling).wait_recv()

    def z_one(p): return copy(p, 0, 0, 8, above)
    def z_two(p): return copy(p, 1, 8, 16, above)

    def even(p, r):
        to = others[r]
        return copy(p, 2 + r, jnp.where(to > x, 0, 16), lax.rem(2 * (to - x) + 16, 16), over_x[r])

    def back(p, r):
        return copy(p, 5 + r, 8, 8 + 2 * (others[r] - x), over_x[r])

    def aside(p, slot): return copy(p, 8 + slot // 2, slot, slot + 1 - 2 * c, sibling)
    def aside_own(p): return copy(p, 8, 16 * c, 1 + 14 * c, sibling)

    def send_up(*planes):
        @pl.when(has_above)
        def _():
            for p in planes:
                z_one(p).start()

    def send_row(p):
        for r in range(3):
            @pl.when(others[r] > x)
            def _():
                even(p, r).start()

        @pl.when(c == 0)
        def _():
            aside_own(p).start()

    def pass_up(p):
        @pl.when(has_below)
        def _():
            arrived(p, 8)

            @pl.when(has_above)
            def _():
                z_two(p).start()

    def back_near(p):
        @pl.when(has_below)
        def _():
            for r in range(3):
                @pl.when(others[r] < x)
                def _():
                    back(p, r).start()
            aside(p, 8).start()

    def back_far(p):
        @pl.when(has_below)
        def _():
            for r in range(3):
                @pl.when(others[r] > x)
                def _():
                    back(p, r).start()

    def send_old(p):
        @pl.when(z > 1)
        def _():
            arrived(p, 16)
            for r in range(3):
                @pl.when(others[r] < x)
                def _():
                    even(p, r).start()

            @pl.when(c == 1)
            def _():
                aside_own(p).start()

    def share(p, slots):
        for slot in slots:
            @pl.when(ctx >= slot)
            def _():
                arrived(p, slot)
                aside(p, slot).start()

    def await_odd(p, slots):
        for slot in slots:
            @pl.when(ctx >= slot)
            def _():
                arrived(p, slot)

    def sent(p):
        @pl.when(has_above)
        def _():
            z_one(p).wait_send()

        @pl.when(has_above & has_below)
        def _():
            z_two(p).wait_send()

        @pl.when(has_below)
        def _():
            for r in range(3):
                back(p, r).wait_send()
        for r in range(3):
            @pl.when((others[r] > x) | (z > 1))
            def _():
                even(p, r).wait_send()

        @pl.when((c == 0) | (z > 1))
        def _():
            aside_own(p).wait_send()
        for slot in range(2, 16, 2):
            @pl.when(ctx >= slot)
            def _():
                aside(p, slot).wait_send()

    def documents():
        base = ctx * TOK
        lens = jnp.broadcast_to(len_ref[...].astype(jnp.float32), (128, 128))
        row = lax.broadcasted_iota(jnp.int32, (128, 128), 0)
        col = lax.broadcasted_iota(jnp.int32, (128, 128), 1)
        ends = jnp.sum(jnp.where(row <= col, lens.T, 0.0), axis=0, keepdims=True)
        here = (base + lax.broadcasted_iota(jnp.int32, (TOK, 128), 0)).astype(jnp.float32)
        start = jnp.max(jnp.where(ends <= here, ends, 0.0), axis=1, keepdims=True)
        offset = start - base.astype(jnp.float32)
        rest = jnp.broadcast_to(jnp.where(offset < 0.0, 0.0, MINUS), (TOK, 128))
        row_bias_ref[...] = rest
        col = lax.broadcasted_iota(jnp.int32, (8, KEYS), 1)
        slot = col // TOK
        at = (col - 2 * TOK * slot).astype(jnp.float32)
        key_bias_ref[...] = jnp.where(at >= offset[:8], 0.0, MINUS)[0:1]
        i = lax.broadcasted_iota(jnp.int32, (TOK, EDGE), 0)
        j = lax.broadcasted_iota(jnp.int32, (TOK, EDGE), 1)
        inside = (j <= i) & (j.astype(jnp.float32) >= offset)
        rest = jnp.concatenate([rest, rest], axis=1) + key_bias_ref[:, :EDGE]
        bias_ref[...] = jnp.where(j < TOK, jnp.where(inside, 0.0, MINUS), rest)

    def clear():
        def one(slot, carry):
            @pl.when(ctx < slot)
            def _():
                for p in range(PLANES):
                    kv[p, rows_of(slot), :] = jnp.zeros((TOK, HEAD), jnp.bfloat16)
            return carry

        lax.fori_loop(1, SLOTS, one, 0)

    def scale_queries():
        def one(h, carry):
            scaled = qv[:, pl.ds(pl.multiple_of(h * HEAD, HEAD), HEAD)].astype(jnp.float32) * SCALE
            high = scaled.astype(jnp.bfloat16)
            qs[rows_of(h), 0:HEAD] = high
            qs[rows_of(h), HEAD:] = (scaled - high.astype(jnp.float32)).astype(jnp.bfloat16)
            return carry

        lax.fori_loop(0, GROUPS * PER_GROUP, one, 0)

    def out_copies(b):
        at = pl.ds(pl.multiple_of(y * 4096 + b * (PART * HEAD), PART * HEAD), PART * HEAD)
        remote = []
        for r in range(3):
            to = over_y[r]
            remote.append(pltpu.make_async_remote_copy(
                src_ref=ob.at[b, pl.ds(pl.multiple_of(to[1] * OWN_TOK, 16), OWN_TOK), :],
                dst_ref=out_ref.at[:, at],
                send_sem=osend_sem.at[b, r], recv_sem=orecv_sem.at[b, r],
                device_id=to, device_id_type=MESH))
        local = pltpu.make_async_copy(
            ob.at[b, pl.ds(pl.multiple_of(y * OWN_TOK, 16), OWN_TOK), :], out_ref.at[:, at],
            olocal_sem.at[b])
        return remote, local

    def score(b, t):
        g = b // PARTS
        kept_at = lax.rem(b, PARTS)
        into = kept_at if t == 0 else PARTS
        q = qs[pl.ds(pl.multiple_of(b * ROWS, ROWS), ROWS), :]
        k = kv[2 * g, t * CHUNK:(t + 1) * CHUNK, :]
        k = jnp.concatenate([k, k], axis=1)
        s = lax.dot_general(q, k, (((1,), (1,)), ((), ())), preferred_element_type=jnp.float32)
        row_bias = jnp.concatenate([row_bias_ref[...]] * PART, axis=0)
        if t == 0:
            edge_bias = jnp.concatenate([bias_ref[...]] * PART, axis=0)
            top = jnp.full((ROWS, 128), MINUS, jnp.float32)
        else:
            top = top_ref[kept_at]
        for u in range(0, CHUNK, 128):
            if t == 0 and u < EDGE:
                bias = edge_bias[:, u:u + 128]
            else:
                bias = row_bias + key_bias_ref[:, t * CHUNK + u:t * CHUNK + u + 128]
            masked = s[:, u:u + 128] + bias
            s_ref[into, :, u:u + 128] = masked
            top = jnp.maximum(top, masked)
        top_ref[kept_at] = top

    def mixed(g, t, frm, m):
        p = jnp.exp2(s_ref[frm] - m).astype(jnp.bfloat16)
        v = kv[2 * g + 1, pl.ds(pl.multiple_of(t * CHUNK, CHUNK), CHUNK), :]
        v = jnp.concatenate([v, jnp.ones_like(v)], axis=1)
        return jnp.dot(p, v, preferred_element_type=jnp.float32)

    def steps(b, table):
        for when, what in table:
            @pl.when(b == when)
            def _():
                what()

    def near_scores(b, carry):
        steps(b, SCORE_STEPS)
        score(b, 0)
        return carry

    def near_mix(b, carry):
        steps(b, MIX_STEPS)
        m = jnp.max(top_ref[b], axis=1, keepdims=True)
        m_ref[b] = jnp.broadcast_to(m, (ROWS, 128))
        near_ref[b] = mixed(0, 0, b, m)
        return carry

    def block(b, carry):
        steps(b, STEPS)
        g = b // PARTS
        kept_at = lax.rem(b, PARTS)

        @pl.when(b >= PARTS)
        def _():
            score(b, 0)
        score(b, 1)
        steps(b, VALUE_STEPS)
        m = jnp.max(top_ref[kept_at], axis=1, keepdims=True)
        before = near_ref[kept_at] * jnp.exp2(m_ref[kept_at] - m)[:, :1]

        def mix(t, total):
            return total + mixed(g, t, jnp.where(t == 0, kept_at, PARTS), m)

        total = lax.fori_loop(
            jnp.where(b < PARTS, 1, 0), 2, mix, jnp.where(b < PARTS, before, 0.0))
        o = (total[:, :HEAD] / total[:, HEAD:]).astype(jnp.bfloat16)
        for h in range(PART):
            ob[b, :, h * HEAD:(h + 1) * HEAD] = o[h * TOK:(h + 1) * TOK]
        remote, local = out_copies(b)
        for one in remote:
            one.start()
        local.start()
        return carry

    near, far = (2, 4, 6), (10, 12, 14)
    odd_near, odd_far = (1, 3, 5, 7), (9, 11, 13, 15)
    SCORE_STEPS = (
        (0, lambda: send_up(2, 3)),
        (1, lambda: (pass_up(1), back_near(1), back_far(0))),
        (2, lambda: send_old(0)),
        (3, lambda: (share(1, near), back_far(1))),
    )
    MIX_STEPS = (
        (0, lambda: (pass_up(2), await_odd(1, odd_near))),
        (1, lambda: (pass_up(3), send_old(1), share(0, far))),
        (3, lambda: (share(1, far), send_row(2), back_near(2), back_far(2))),
    )
    STEPS = (
        (0, lambda: (await_odd(0, odd_far), send_old(2))),
        (1, lambda: send_old(3)),
        (2, lambda: share(2, near + far)),
        (3, lambda: share(3, near + far)),
        (4, lambda: await_odd(2, odd_near + odd_far)),
    )
    VALUE_STEPS = (
        (0, lambda: (await_odd(1, odd_far), send_row(3), back_near(3), back_far(3))),
        (4, lambda: await_odd(3, odd_near + odd_far)),
    )

    send_row(0)
    documents()
    clear()

    @pl.when(has_above)
    def _():
        pl.semaphore_wait(above_sem, 1)

    send_up(0, 1)
    q_load.wait()
    scale_queries()
    pass_up(0)
    back_near(0)
    send_row(1)
    share(0, near)
    await_odd(0, odd_near)
    lax.fori_loop(0, PARTS, near_scores, 0)
    lax.fori_loop(0, PARTS, near_mix, 0)
    lax.fori_loop(0, BLOCKS, block, 0)

    def finish(b, carry):
        remote, local = out_copies(b)
        for one in remote:
            one.wait()
        local.wait()
        return carry

    lax.fori_loop(0, BLOCKS, finish, 0)
    for p in range(PLANES):
        sent(p)


def per_device(queries, keys, values, doc_lengths):
    hbm = pl.BlockSpec(memory_space=pl.ANY)
    bf16, f32 = jnp.bfloat16, jnp.float32
    return pl.pallas_call(
        kernel,
        out_shape=pltpu.VMEM((OWN_TOK, 4 * queries.shape[1]), bf16),
        in_specs=[hbm, hbm, hbm, pl.BlockSpec(memory_space=pltpu.VMEM)],
        out_specs=pl.BlockSpec(memory_space=pltpu.VMEM),
        scratch_shapes=[
            pltpu.VMEM((PLANES, (SLOTS + 1) * TOK, HEAD), bf16),
            pltpu.VMEM((PARTS + 1, ROWS, CHUNK), f32),
            pltpu.VMEM((PARTS, ROWS, 128), f32),
            pltpu.VMEM((PARTS, ROWS, 128), f32),
            pltpu.VMEM((PARTS, ROWS, 2 * HEAD), f32),
            pltpu.VMEM((TOK, 4096), bf16),
            pltpu.VMEM((GROUPS * PER_GROUP * TOK, 2 * HEAD), bf16),
            pltpu.VMEM((BLOCKS, TOK, PART * HEAD), bf16),
            pltpu.VMEM((TOK, 128), f32),
            pltpu.VMEM((1, KEYS), f32),
            pltpu.VMEM((TOK, EDGE), f32),
            pltpu.SemaphoreType.DMA((PLANES + 1,)),
            pltpu.SemaphoreType.REGULAR,
            pltpu.SemaphoreType.DMA((PLANES, 16)),
            pltpu.SemaphoreType.DMA((PLANES, SLOTS + 1)),
            pltpu.SemaphoreType.DMA((BLOCKS, 3)),
            pltpu.SemaphoreType.DMA((BLOCKS, 3)),
            pltpu.SemaphoreType.DMA((BLOCKS,)),
        ],
        compiler_params=pltpu.CompilerParams(
            collective_id=0, has_side_effects=True, vmem_limit_bytes=56 << 20),
    )(queries, keys, values, doc_lengths.reshape(1, 128))


def solution(mesh):
    placed = (P("ctx", "head"), P("ctx", "head"), P("ctx", "head"), P())
    return jax.shard_map(
        per_device, mesh=mesh, in_specs=placed, out_specs=P(("ctx", "head"), None), check_vma=False
    )
```

time: 69.7 us -> 59.5 us (0.85)
  the two profiles are of different devices: /device:TPU:1 before, /device:TPU:128 now
where the time goes in v3:
time: 59.5 us; the launch traced here: 59.4 us
  Pallas kernels  58.2 us (98%)
  local copies, waits for them, and re-layouts  1.15 us (2%)
    pallas_call x1, Pallas kernels, per_device(): pl.pallas_call(kernel, out_shape=pltpu.VMEM((OWN_TOK, 4 * queries.shape[1...  58.2 us

profile of v3, /device:TPU:128, one launch (start us, length us, event | category | flops | bytes accessed | tf_op | source)
XLA Modules:
  0.0 59.4 jit_solution(17952299690007751875)
XLA Ops:
  0.0 58.2 %shard_map.46 = bf16[48,16384]{1,0:T(8,128)(2,1)S(1)} custom-call(bf16[192,4096]{1,0:T(8,128)(2,1)} %q_hbm.1, bf16[192,256]{1,0:T(8,128)(2,1)} %k_hbm.1, bf16[192,256]{1,0:T(8,128)(2,1)} %v_hbm.1, s32[1,128]{1,0:T(1,128)} %bitcast.1), custom_call_target="tpu_custom_call" | custom-call | tf_op jit(solution)/shard_map/pallas_call | solution.py:390
  58.2 1.1 %copy.6 = bf16[48,16384]{1,0:T(8,128)(2,1)} copy(bf16[48,16384]{1,0:T(8,128)(2,1)S(1)} %shard_map.46) | data formatting | bytes 3145728

commit v4 on v3

--- a/solution.py
+++ b/solution.py
@@ -26,6 +26,7 @@
 
 
 PLANES = 2 * GROUPS
+MOVES = 3
 
 
 def rows_of(slot):
@@ -34,7 +35,7 @@
 
 def kernel(
     q_hbm, k_hbm, v_hbm, len_ref, out_ref,
-    kv, s_ref, top_ref, m_ref, near_ref, qv, qs, ob, row_bias_ref, key_bias_ref, bias_ref,
+    kv, s_ref, top_ref, m_ref, near_ref, total_ref, qv, qs, ob, row_bias_ref, key_bias_ref, bias_ref,
     in_sem, above_sem, send_sem, recv_sem, osend_sem, orecv_sem, olocal_sem,
 ):
     ctx = lax.axis_index("ctx")
@@ -63,6 +64,8 @@
     barrier = pltpu.get_barrier_semaphore()
     above, below = place(z + 1, x, c), place(z - 1, x, c)
     has_above, has_below = z < 7, z > 0
+    aslant = [place(z + 1, to, c) for to in others]
+    from_slant = [place(z - 1, to, c) for to in others]
     partners = [sibling] + over_x + over_y
     for partner in partners:
         pl.semaphore_signal(barrier, inc=1, device_id=partner, device_id_type=MESH)
@@ -70,19 +73,28 @@
     @pl.when(has_above)
     def _():
         pl.semaphore_signal(barrier, inc=1, device_id=above, device_id_type=MESH)
-
-    pl.semaphore_wait(barrier, len(partners) + jnp.where(has_below, 1, 0))
+        for r in range(3):
+            @pl.when(others[r] < x)
+            def _():
+                pl.semaphore_signal(barrier, inc=1, device_id=aslant[r], device_id_type=MESH)
+
+    pl.semaphore_wait(barrier, len(partners) + jnp.where(has_below, 4 - x, 0))
 
     @pl.when(has_below)
     def _():
         pl.semaphore_signal(above_sem, inc=1, device_id=below, device_id_type=MESH)
+        for r in range(3):
+            @pl.when(others[r] > x)
+            def _():
+                pl.semaphore_signal(above_sem, inc=1, device_id=from_slant[r], device_id_type=MESH)
 
     for load in loads:
         load.wait()
 
     def copy(p, index, src, dst, target):
+        planes = pl.ds(p, 1 if p < 2 else 2)
         return pltpu.make_async_remote_copy(
-            src_ref=kv.at[p, rows_of(src), :], dst_ref=kv.at[p, rows_of(dst), :],
+            src_ref=kv.at[planes, rows_of(src), :], dst_ref=kv.at[planes, rows_of(dst), :],
             send_sem=send_sem.at[p, index], recv_sem=recv_sem.at[p, dst],
             device_id=target, device_id_type=MESH)
 
@@ -99,6 +111,9 @@
     def back(p, r):
         return copy(p, 5 + r, 8, 8 + 2 * (others[r] - x), over_x[r])
 
+    def slanted(r):
+        return copy(0, 5 + r, 0, 8 + 2 * (others[r] - x), aslant[r])
+
     def aside(p, slot): return copy(p, 8 + slot // 2, slot, slot + 1 - 2 * c, sibling)
     def aside_own(p): return copy(p, 8, 16 * c, 1 + 14 * c, sibling)
 
@@ -108,33 +123,42 @@
             for p in planes:
                 z_one(p).start()
 
-    def send_row(p):
-        for r in range(3):
-            @pl.when(others[r] > x)
-            def _():
-                even(p, r).start()
-
-        @pl.when(c == 0)
-        def _():
-            aside_own(p).start()
-
-    def pass_up(p):
-        @pl.when(has_below)
-        def _():
-            arrived(p, 8)
-
-            @pl.when(has_above)
-            def _():
-                z_two(p).start()
-
-    def back_near(p):
-        @pl.when(has_below)
+    def send_slanted():
+        @pl.when(has_above)
         def _():
             for r in range(3):
                 @pl.when(others[r] < x)
                 def _():
-                    back(p, r).start()
+                    slanted(r).start()
+
+    def send_row(p):
+        for r in range(3):
+            @pl.when(others[r] > x)
+            def _():
+                even(p, r).start()
+
+        @pl.when(c == 0)
+        def _():
+            aside_own(p).start()
+
+    def pass_up(p):
+        @pl.when(has_below)
+        def _():
+            arrived(p, 8)
+
+            @pl.when(has_above)
+            def _():
+                z_two(p).start()
+
+    def back_near(p):
+        @pl.when(has_below)
+        def _():
             aside(p, 8).start()
+            if p > 0:
+                for r in range(3):
+                    @pl.when(others[r] < x)
+                    def _():
+                        back(p, r).start()
 
     def back_far(p):
         @pl.when(has_below)
@@ -179,9 +203,11 @@
         def _():
             z_two(p).wait_send()
 
-        @pl.when(has_below)
-        def _():
-            for r in range(3):
+        for r in range(3):
+            by_slant = others[r] < x if p == 0 else False
+
+            @pl.when(has_above & by_slant | has_below & jnp.logical_not(by_slant))
+            def _():
                 back(p, r).wait_send()
         for r in range(3):
             @pl.when((others[r] > x) | (z > 1))
@@ -237,48 +263,49 @@
 
         lax.fori_loop(0, GROUPS * PER_GROUP, one, 0)
 
-    def out_copies(b):
-        at = pl.ds(pl.multiple_of(y * 4096 + b * (PART * HEAD), PART * HEAD), PART * HEAD)
-        remote = []
-        for r in range(3):
-            to = over_y[r]
-            remote.append(pltpu.make_async_remote_copy(
-                src_ref=ob.at[b, pl.ds(pl.multiple_of(to[1] * OWN_TOK, 16), OWN_TOK), :],
-                dst_ref=out_ref.at[:, at],
-                send_sem=osend_sem.at[b, r], recv_sem=orecv_sem.at[b, r],
-                device_id=to, device_id_type=MESH))
-        local = pltpu.make_async_copy(
-            ob.at[b, pl.ds(pl.multiple_of(y * OWN_TOK, 16), OWN_TOK), :], out_ref.at[:, at],
-            olocal_sem.at[b])
-        return remote, local
-
-    def score(b, t):
+    def out_copies(b, head, count):
+        width = count * HEAD
+        cols = pl.ds(head * HEAD, width)
+        at = pl.ds(pl.multiple_of(y * 4096 + (b * PART + head) * HEAD, width), width)
+
+        def part(to):
+            return ob.at[b, pl.ds(pl.multiple_of(to * OWN_TOK, 16), OWN_TOK), cols]
+
+        copies = [pltpu.make_async_copy(part(y), out_ref.at[:, at], olocal_sem)]
+        for r in range(3):
+            copies.append(pltpu.make_async_remote_copy(
+                src_ref=part(over_y[r][1]), dst_ref=out_ref.at[:, at],
+                send_sem=osend_sem.at[r], recv_sem=orecv_sem.at[r],
+                device_id=over_y[r], device_id_type=MESH))
+        return copies
+
+    def score(b, lo, hi):
         g = b // PARTS
         kept_at = lax.rem(b, PARTS)
-        into = kept_at if t == 0 else PARTS
+        into = kept_at if lo < CHUNK else PARTS
         q = qs[pl.ds(pl.multiple_of(b * ROWS, ROWS), ROWS), :]
-        k = kv[2 * g, t * CHUNK:(t + 1) * CHUNK, :]
+        k = kv[2 * g, lo:hi, :]
         k = jnp.concatenate([k, k], axis=1)
         s = lax.dot_general(q, k, (((1,), (1,)), ((), ())), preferred_element_type=jnp.float32)
         row_bias = jnp.concatenate([row_bias_ref[...]] * PART, axis=0)
-        if t == 0:
+        if lo == 0:
             edge_bias = jnp.concatenate([bias_ref[...]] * PART, axis=0)
             top = jnp.full((ROWS, 128), MINUS, jnp.float32)
         else:
             top = top_ref[kept_at]
-        for u in range(0, CHUNK, 128):
-            if t == 0 and u < EDGE:
+        for u in range(lo, hi, 128):
+            if u < EDGE:
                 bias = edge_bias[:, u:u + 128]
             else:
-                bias = row_bias + key_bias_ref[:, t * CHUNK + u:t * CHUNK + u + 128]
-            masked = s[:, u:u + 128] + bias
-            s_ref[into, :, u:u + 128] = masked
+                bias = row_bias + key_bias_ref[:, u:u + 128]
+            masked = s[:, u - lo:u - lo + 128] + bias
+            s_ref[into, :, u % CHUNK:u % CHUNK + 128] = masked
             top = jnp.maximum(top, masked)
         top_ref[kept_at] = top
 
-    def mixed(g, t, frm, m):
-        p = jnp.exp2(s_ref[frm] - m).astype(jnp.bfloat16)
-        v = kv[2 * g + 1, pl.ds(pl.multiple_of(t * CHUNK, CHUNK), CHUNK), :]
+    def mixed(g, t, scores, m):
+        p = jnp.exp2(scores - m).astype(jnp.bfloat16)
+        v = kv[2 * g + 1, t * CHUNK:(t + 1) * CHUNK, :]
         v = jnp.concatenate([v, jnp.ones_like(v)], axis=1)
         return jnp.dot(p, v, preferred_element_type=jnp.float32)
 
@@ -288,79 +315,87 @@
             def _():
                 what()
 
-    def near_scores(b, carry):
-        steps(b, SCORE_STEPS)
-        score(b, 0)
-        return carry
+    def scores(table, lo, hi):
+        def one(b, carry):
+            steps(b, table)
+            score(b, lo, hi)
+            return carry
+        return one
 
     def near_mix(b, carry):
         steps(b, MIX_STEPS)
         m = jnp.max(top_ref[b], axis=1, keepdims=True)
         m_ref[b] = jnp.broadcast_to(m, (ROWS, 128))
-        near_ref[b] = mixed(0, 0, b, m)
+        near_ref[b] = mixed(0, 0, s_ref[b], m)
         return carry
 
     def block(b, carry):
         steps(b, STEPS)
         g = b // PARTS
         kept_at = lax.rem(b, PARTS)
+        score(b, CHUNK, KEYS)
+        steps(b, VALUE_STEPS)
+
+        @pl.when(b < PARTS)
+        def _():
+            m = jnp.max(top_ref[kept_at], axis=1, keepdims=True)
+            scale = jnp.exp2(m_ref[kept_at] - m)
+            total_ref[:, :HEAD] = near_ref[kept_at, :, :HEAD] * scale
+            total_ref[:, HEAD:] = near_ref[kept_at, :, HEAD:] * scale
 
         @pl.when(b >= PARTS)
         def _():
-            score(b, 0)
-        score(b, 1)
-        steps(b, VALUE_STEPS)
+            m = jnp.max(top_ref[kept_at], axis=1, keepdims=True)
+            total_ref[...] = mixed(g, 0, s_ref[kept_at], m)
+
         m = jnp.max(top_ref[kept_at], axis=1, keepdims=True)
-        before = near_ref[kept_at] * jnp.exp2(m_ref[kept_at] - m)[:, :1]
-
-        def mix(t, total):
-            return total + mixed(g, t, jnp.where(t == 0, kept_at, PARTS), m)
-
-        total = lax.fori_loop(
-            jnp.where(b < PARTS, 1, 0), 2, mix, jnp.where(b < PARTS, before, 0.0))
+        total = total_ref[...] + mixed(g, 1, s_ref[PARTS], m)
         o = (total[:, :HEAD] / total[:, HEAD:]).astype(jnp.bfloat16)
         for h in range(PART):
             ob[b, :, h * HEAD:(h + 1) * HEAD] = o[h * TOK:(h + 1) * TOK]
-        remote, local = out_copies(b)
-        for one in remote:
+        for one in out_copies(b, 0, PART):
             one.start()
-        local.start()
         return carry
 
     near, far = (2, 4, 6), (10, 12, 14)
     odd_near, odd_far = (1, 3, 5, 7), (9, 11, 13, 15)
     SCORE_STEPS = (
-        (0, lambda: send_up(2, 3)),
-        (1, lambda: (pass_up(1), back_near(1), back_far(0))),
+        (0, lambda: (back_far(0), send_up(2))),
+        (1, lambda: (pass_up(1), back_near(1))),
         (2, lambda: send_old(0)),
         (3, lambda: (share(1, near), back_far(1))),
     )
     MIX_STEPS = (
-        (0, lambda: (pass_up(2), await_odd(1, odd_near))),
-        (1, lambda: (pass_up(3), send_old(1), share(0, far))),
-        (3, lambda: (share(1, far), send_row(2), back_near(2), back_far(2))),
+        (0, lambda: (await_odd(1, odd_near), send_row(2))),
+        (1, lambda: (send_old(1), share(0, far))),
+        (2, lambda: (pass_up(2), back_near(2))),
+        (3, lambda: (share(1, far), back_far(2))),
     )
     STEPS = (
-        (0, lambda: (await_odd(0, odd_far), send_old(2))),
-        (1, lambda: send_old(3)),
-        (2, lambda: share(2, near + far)),
-        (3, lambda: share(3, near + far)),
-        (4, lambda: await_odd(2, odd_near + odd_far)),
+        (0, lambda: await_odd(0, odd_far)),
+        (1, lambda: send_old(2)),
+        (3, lambda: share(2, near)),
+        (4, lambda: await_odd(2, odd_far)),
     )
     VALUE_STEPS = (
-        (0, lambda: (await_odd(1, odd_far), send_row(3), back_near(3), back_far(3))),
-        (4, lambda: await_odd(3, odd_near + odd_far)),
+        (0, lambda: await_odd(1, odd_far)),
+    )
+    LATER_STEPS = (
+        (4, lambda: await_odd(2, odd_near)),
+        (5, lambda: share(2, far)),
     )
 
     send_row(0)
+
+    @pl.when(has_above)
+    def _():
+        pl.semaphore_wait(above_sem, x + 1)
+
+    send_up(0)
+    send_slanted()
+    send_up(1)
     documents()
     clear()
-
-    @pl.when(has_above)
-    def _():
-        pl.semaphore_wait(above_sem, 1)
-
-    send_up(0, 1)
     q_load.wait()
     scale_queries()
     pass_up(0)
@@ -368,19 +403,21 @@
     send_row(1)
     share(0, near)
     await_odd(0, odd_near)
-    lax.fori_loop(0, PARTS, near_scores, 0)
+    lax.fori_loop(0, PARTS, scores(SCORE_STEPS, 0, CHUNK), 0)
     lax.fori_loop(0, PARTS, near_mix, 0)
-    lax.fori_loop(0, BLOCKS, block, 0)
-
-    def finish(b, carry):
-        remote, local = out_copies(b)
-        for one in remote:
-            one.wait()
-        local.wait()
-        return carry
-
-    lax.fori_loop(0, BLOCKS, finish, 0)
-    for p in range(PLANES):
+    lax.fori_loop(0, PARTS, block, 0)
+    lax.fori_loop(PARTS, BLOCKS, scores(LATER_STEPS, 0, CHUNK), 0)
+    lax.fori_loop(PARTS, BLOCKS, block, 0)
+
+    mine = out_ref.at[:, pl.ds(pl.multiple_of(y * 4096, 4096), 4096)]
+    for r in range(3):
+        every = pltpu.make_async_remote_copy(
+            src_ref=mine, dst_ref=mine, send_sem=osend_sem.at[r], recv_sem=orecv_sem.at[r],
+            device_id=over_y[r], device_id_type=MESH)
+        every.wait_send()
+        every.wait_recv()
+    pltpu.make_async_copy(mine, mine, olocal_sem).wait()
+    for p in range(MOVES):
         sent(p)
 
 
@@ -398,6 +435,7 @@
             pltpu.VMEM((PARTS, ROWS, 128), f32),
             pltpu.VMEM((PARTS, ROWS, 128), f32),
             pltpu.VMEM((PARTS, ROWS, 2 * HEAD), f32),
+            pltpu.VMEM((ROWS, 2 * HEAD), f32),
             pltpu.VMEM((TOK, 4096), bf16),
             pltpu.VMEM((GROUPS * PER_GROUP * TOK, 2 * HEAD), bf16),
             pltpu.VMEM((BLOCKS, TOK, PART * HEAD), bf16),
@@ -406,11 +444,11 @@
             pltpu.VMEM((TOK, EDGE), f32),
             pltpu.SemaphoreType.DMA((PLANES + 1,)),
             pltpu.SemaphoreType.REGULAR,
-            pltpu.SemaphoreType.DMA((PLANES, 16)),
-            pltpu.SemaphoreType.DMA((PLANES, SLOTS + 1)),
-            pltpu.SemaphoreType.DMA((BLOCKS, 3)),
-            pltpu.SemaphoreType.DMA((BLOCKS, 3)),
-            pltpu.SemaphoreType.DMA((BLOCKS,)),
+            pltpu.SemaphoreType.DMA((MOVES, 16)),
+            pltpu.SemaphoreType.DMA((MOVES, SLOTS + 1)),
+            pltpu.SemaphoreType.DMA((3,)),
+            pltpu.SemaphoreType.DMA((3,)),
+            pltpu.SemaphoreType.DMA,
         ],
         compiler_params=pltpu.CompilerParams(
             collective_id=0, has_side_effects=True, vmem_limit_bytes=56 << 20),

time: 59.5 us -> 56.3 us (0.946)
  Pallas kernels: 58.2 us -> 55 us
    pallas_call x1, Pallas kernels: 58.2 us -> 55 us  [per_device(): pl.pallas_call(kernel, out_shape=pltpu.VMEM((OWN_TOK, 4 * queries.shape[1...]
where the time goes in v4:
time: 56.3 us; the launch traced here: 56.2 us
  Pallas kernels  55 us (98%)
  local copies, waits for them, and re-layouts  1.15 us (2%)
    pallas_call x1, Pallas kernels, per_device(): pl.pallas_call(kernel, out_shape=pltpu.VMEM((OWN_TOK, 4 * queries.shape[1...  55 us
    unnamed x1, local copies, waits for them, and re-layouts  1.15 us

profile of v4, /device:TPU:128, one launch (start us, length us, event | category | flops | bytes accessed | tf_op | source)
XLA Modules:
  0.0 56.2 jit_solution(11232351012162575517)
XLA Ops:
  0.0 55.0 %shard_map.46 = bf16[48,16384]{1,0:T(8,128)(2,1)S(1)} custom-call(bf16[192,4096]{1,0:T(8,128)(2,1)} %q_hbm.1, bf16[192,256]{1,0:T(8,128)(2,1)} %k_hbm.1, bf16[192,256]{1,0:T(8,128)(2,1)} %v_hbm.1, s32[1,128]{1,0:T(1,128)} %bitcast.1), custom_call_target="tpu_custom_call" | custom-call | tf_op jit(solution)/shard_map/pallas_call | solution.py:427
  55.0 1.1 %copy.6 = bf16[48,16384]{1,0:T(8,128)(2,1)} copy(bf16[48,16384]{1,0:T(8,128)(2,1)S(1)} %shard_map.46) | data formatting | bytes 3145728

commit v5 on v4

--- a/solution.py
+++ b/solution.py
@@ -36,7 +36,7 @@
 def kernel(
     q_hbm, k_hbm, v_hbm, len_ref, out_ref,
     kv, s_ref, top_ref, m_ref, near_ref, total_ref, qv, qs, ob, row_bias_ref, key_bias_ref, bias_ref,
-    in_sem, above_sem, send_sem, recv_sem, osend_sem, orecv_sem, olocal_sem,
+    in_sem, send_sem, recv_sem, osend_sem, orecv_sem, olocal_sem,
 ):
     ctx = lax.axis_index("ctx")
     y = lax.axis_index("head")
@@ -78,15 +78,16 @@
             def _():
                 pl.semaphore_signal(barrier, inc=1, device_id=aslant[r], device_id_type=MESH)
 
-    pl.semaphore_wait(barrier, len(partners) + jnp.where(has_below, 4 - x, 0))
-
     @pl.when(has_below)
     def _():
-        pl.semaphore_signal(above_sem, inc=1, device_id=below, device_id_type=MESH)
+        pl.semaphore_signal(barrier, inc=1, device_id=below, device_id_type=MESH)
         for r in range(3):
             @pl.when(others[r] > x)
             def _():
-                pl.semaphore_signal(above_sem, inc=1, device_id=from_slant[r], device_id_type=MESH)
+                pl.semaphore_signal(barrier, inc=1, device_id=from_slant[r], device_id_type=MESH)
+
+    pl.semaphore_wait(
+        barrier, len(partners) + jnp.where(has_below, 4 - x, 0) + jnp.where(has_above, x + 1, 0))
 
     for load in loads:
         load.wait()
@@ -385,14 +386,9 @@
         (5, lambda: share(2, far)),
     )
 
-    send_row(0)
-
-    @pl.when(has_above)
-    def _():
-        pl.semaphore_wait(above_sem, x + 1)
-
     send_up(0)
     send_slanted()
+    send_row(0)
     send_up(1)
     documents()
     clear()
@@ -443,7 +439,6 @@
             pltpu.VMEM((1, KEYS), f32),
             pltpu.VMEM((TOK, EDGE), f32),
             pltpu.SemaphoreType.DMA((PLANES + 1,)),
-            pltpu.SemaphoreType.REGULAR,
             pltpu.SemaphoreType.DMA((MOVES, 16)),
             pltpu.SemaphoreType.DMA((MOVES, SLOTS + 1)),
             pltpu.SemaphoreType.DMA((3,)),

time: 56.3 us -> 54.1 us (0.961)
  Pallas kernels: 55 us -> 52.8 us
    pallas_call x1, Pallas kernels: 55 us -> 52.8 us  [per_device(): pl.pallas_call(kernel, out_shape=pltpu.VMEM((OWN_TOK, 4 * queries.shape[1...]
where the time goes in v5:
time: 54.1 us; the launch traced here: 54 us
  Pallas kernels  52.8 us (98%)
  local copies, waits for them, and re-layouts  1.15 us (2%)
    pallas_call x1, Pallas kernels, per_device(): pl.pallas_call(kernel, out_shape=pltpu.VMEM((OWN_TOK, 4 * queries.shape[1...  52.8 us
    unnamed x1, local copies, waits for them, and re-layouts  1.15 us

profile of v5, /device:TPU:128, one launch (start us, length us, event | category | flops | bytes accessed | tf_op | source)
XLA Modules:
  0.0 54.0 jit_solution(12037142970482505695)
XLA Ops:
  0.0 52.8 %shard_map.46 = bf16[48,16384]{1,0:T(8,128)(2,1)S(1)} custom-call(bf16[192,4096]{1,0:T(8,128)(2,1)} %q_hbm.1, bf16[192,256]{1,0:T(8,128)(2,1)} %k_hbm.1, bf16[192,256]{1,0:T(8,128)(2,1)} %v_hbm.1, s32[1,128]{1,0:T(1,128)} %bitcast.1), custom_call_target="tpu_custom_call" | custom-call | tf_op jit(solution)/shard_map/pallas_call | solution.py:423
  52.8 1.1 %copy.6 = bf16[48,16384]{1,0:T(8,128)(2,1)} copy(bf16[48,16384]{1,0:T(8,128)(2,1)S(1)} %shard_map.46) | data formatting | bytes 3145728
